TPU v7x, 32 devices: a whole 2x2x4 slice. The times are simulated.
32 devices in a mesh: dp: 8 (over y, x, core), seq: 4 (over z).
Axes of the slice: x: 2, y: 2, z: 4, core: 2. Of those that a mesh axis runs over, the one named last changes fastest.
Arguments:
- x_short: bfloat16 [16, 512, 512], P('dp', 'seq'), may hold values from -6 to 6
- order_short: int32 [512], P('seq'), may hold values from 0 to 511, as said below
- x_long: bfloat16 [24, 1024, 512], P('dp', 'seq'), may hold values from -6 to 6
- order_long: int32 [1024], P('seq'), may hold values from 0 to 1023, as said below
- w_query: bfloat16 [512, 512], replicated, may hold values from -0.25 to 0.25
- w_key: bfloat16 [512, 512], replicated, may hold values from -0.25 to 0.25
- w_value: bfloat16 [512, 512], replicated, may hold values from -0.25 to 0.25
- w_out: bfloat16 [512, 512], replicated, may hold values from -2 to 2
- b_out: float32 [512], replicated, may hold values from -2 to 2
- alphas: float32 [2], replicated, may hold values from 0.5 to 1.5
- w_up: bfloat16 [512, 2048], replicated, may hold values from -0.25 to 0.25
- b_up: float32 [2048], replicated, may hold values from -3 to 3
- w_down: bfloat16 [2048, 512], replicated, may hold values from -0.125 to 0.125
- b_down: float32 [512], replicated, may hold values from -2 to 2
- cot_short: bfloat16 [16, 512, 512], P('dp', 'seq'), may hold values from -6 to 6
- cot_long: bfloat16 [24, 1024, 512], P('dp', 'seq'), may hold values from -6 to 6
Outputs:
- out_short: bfloat16 [16, 512, 512], P('dp', 'seq')
- out_long: bfloat16 [24, 1024, 512], P('dp', 'seq')
- dx_short: float32 [16, 512, 512], P('dp', 'seq')
- dx_long: float32 [24, 1024, 512], P('dp', 'seq')
- g_query: float32 [512, 512], replicated
- g_key: float32 [512, 512], replicated
- g_value: float32 [512, 512], replicated
- g_out: float32 [512, 512], replicated
- g_bout: float32 [512], replicated
- g_alphas: float32 [2], replicated
- g_up: float32 [512, 2048], replicated
- g_bup: float32 [2048], replicated
- g_down: float32 [2048, 512], replicated
- g_bdown: float32 [512], replicated
Inputs may be any that keep to these rules, and one draw needn't show every extreme that they name: A permutation of paired runs: stored row j of every short sequence is the token at position order_short[j]. Positions fall into 2 * 4 runs of 512 // (2 * 4) consecutive positions; the k-th block of 512 // 4 stored rows holds in its first half the run c and in its second half the run 2 * 4 - 1 - c, for some c that differs from block to block; within a half the rows may be in any order. The same for the long sequences: stored row j is the token at position order_long[j], with runs of 1024 // (2 * 4) positions paired as above.
All inputs are finite; a program needn't handle non-finite values.
Results may differ from a plain program's by a relative error of at most 0.012.
The roundings to bfloat16 on the way count: a program that leaves them out, or rounds other values in their place, can miss the bound.
Values may be sent and summed in bfloat16 or wider, within the bound.
No kernel may reach another device: no remote copies, remote signals or barrier semaphores. Data moves between devices by JAX's collectives and lax.ppermute only.
A program may use at most 256 MiB of HBM per device.

v0:
```python
import jax
import jax.numpy as jnp
from jax import lax
from jax.sharding import PartitionSpec as P

HEADS = 8
HEAD_DIM = 64


def heads_view(values):
    return values.reshape(values.shape[0], values.shape[1], HEADS, HEAD_DIM)


def project(inputs, weight):
    flat_in = inputs.reshape(-1, inputs.shape[-1])
    product = jnp.dot(flat_in, weight, preferred_element_type=jnp.float32)
    return product.astype(jnp.bfloat16).reshape(inputs.shape[0], inputs.shape[1], weight.shape[1])


def masked_scores(queries, key_rows, query_pos, key_pos):
    scores = jnp.einsum(
        "sqhe,skhe->shqk",
        heads_view(queries),
        heads_view(key_rows),
        preferred_element_type=jnp.float32,
    ) * HEAD_DIM ** (-0.5)
    allowed = query_pos[:, None] >= key_pos[None, :]
    return jnp.where(allowed, scores, -1e30)


def attend(queries, key_all, value_all, query_pos, key_pos):
    scores = masked_scores(queries, key_all, query_pos, key_pos)
    row_top = jnp.max(scores, axis=-1, keepdims=True)
    raised = jnp.exp(scores - row_top)
    row_total = jnp.sum(raised, axis=-1, keepdims=True)
    soft_low = (raised / row_total).astype(jnp.bfloat16)
    mixture = jnp.einsum(
        "shqk,skhe->sqhe", soft_low, heads_view(value_all), preferred_element_type=jnp.float32
    )
    attended = mixture.astype(jnp.bfloat16).reshape(queries.shape)
    log_total = (row_top + jnp.log(row_total))[..., 0]
    return (attended, log_total)


def query_grads(queries, key_all, value_all, query_pos, key_pos, log_total, grad_att):
    scores = masked_scores(queries, key_all, query_pos, key_pos)
    soft_full = jnp.exp(scores - log_total[..., None])
    grad_soft = jnp.einsum(
        "sqhe,skhe->shqk",
        heads_view(grad_att),
        heads_view(value_all),
        preferred_element_type=jnp.float32,
    )
    inner_sum = jnp.sum(soft_full * grad_soft, axis=-1)
    grad_score = (soft_full * (grad_soft - inner_sum[..., None])).astype(jnp.bfloat16)
    grad_query = jnp.einsum(
        "shqk,skhe->sqhe", grad_score, heads_view(key_all), preferred_element_type=jnp.float32
    ) * HEAD_DIM ** (-0.5)
    return (
        soft_full,
        grad_score,
        inner_sum,
        grad_query.astype(jnp.bfloat16).reshape(queries.shape),
    )


def key_partials(queries, grad_att, soft_full, grad_score):
    grad_key = jnp.einsum(
        "shqk,sqhe->skhe", grad_score, heads_view(queries), preferred_element_type=jnp.float32
    ) * HEAD_DIM ** (-0.5)
    grad_value = jnp.einsum(
        "shqk,sqhe->skhe",
        soft_full.astype(jnp.bfloat16),
        heads_view(grad_att),
        preferred_element_type=jnp.float32,
    )
    out_shape = (queries.shape[0], grad_key.shape[1], queries.shape[2])
    return (grad_key.reshape(out_shape), grad_value.reshape(out_shape))


def dense_forward(inputs, attended, dense):
    w_out, b_out, alphas, w_up, b_up, w_down, b_down = dense
    flat_in = inputs.reshape(-1, inputs.shape[-1])
    flat_att = attended.reshape(flat_in.shape)
    branch = jnp.dot(flat_att, w_out, preferred_element_type=jnp.float32) + b_out
    middle = flat_in.astype(jnp.float32) + alphas[0] * branch
    middle_low = middle.astype(jnp.bfloat16)
    hidden = jnp.dot(middle_low, w_up, preferred_element_type=jnp.float32) + b_up
    active = jax.nn.gelu(hidden).astype(jnp.bfloat16)
    feed_out = jnp.dot(active, w_down, preferred_element_type=jnp.float32) + b_down
    final = middle + alphas[1] * feed_out
    return (branch, middle_low, hidden, active, feed_out, final)


def dense_backward(cotangent, attended, kept, dense):
    w_out, b_out, alphas, w_up, b_up, w_down, b_down = dense
    branch, middle_low, hidden, active, feed_out, final = kept
    grad_final = cotangent.reshape(final.shape).astype(jnp.float32)
    alpha_feed = jnp.sum(feed_out * grad_final)
    grad_feed = (alphas[1] * grad_final).astype(jnp.bfloat16)
    bias_down = jnp.sum(grad_feed.astype(jnp.float32), axis=0)
    grad_down = jnp.dot(active.T, grad_feed, preferred_element_type=jnp.float32)
    grad_active = jnp.dot(grad_feed, w_down.T, preferred_element_type=jnp.float32)
    unused, gelu_back = jax.vjp(jax.nn.gelu, hidden)
    grad_hidden = gelu_back(grad_active)[0].astype(jnp.bfloat16)
    bias_up = jnp.sum(grad_hidden.astype(jnp.float32), axis=0)
    grad_up = jnp.dot(middle_low.T, grad_hidden, preferred_element_type=jnp.float32)
    grad_middle = grad_final + jnp.dot(grad_hidden, w_up.T, preferred_element_type=jnp.float32)
    alpha_branch = jnp.sum(branch * grad_middle)
    grad_branch = (alphas[0] * grad_middle).astype(jnp.bfloat16)
    flat_att = attended.reshape(-1, attended.shape[-1])
    bias_out = jnp.sum(grad_branch.astype(jnp.float32), axis=0)
    grad_out = jnp.dot(flat_att.T, grad_branch, preferred_element_type=jnp.float32)
    grad_att = (
        jnp.dot(grad_branch, w_out.T, preferred_element_type=jnp.float32)
        .astype(jnp.bfloat16)
        .reshape(attended.shape)
    )
    grads = (
        grad_out,
        bias_out,
        jnp.stack([alpha_branch, alpha_feed]),
        grad_up,
        bias_up,
        grad_down,
        bias_down,
    )
    return (grad_middle, grad_att, grads)


def input_grads(inputs, grad_middle, grad_query, grad_key, grad_value, projections):
    w_query, w_key, w_value = projections
    flat_in = inputs.reshape(-1, inputs.shape[-1])
    query_flat = grad_query.reshape(flat_in.shape)
    key_flat = grad_key.reshape(flat_in.shape)
    value_flat = grad_value.reshape(flat_in.shape)
    grad_input = grad_middle + jnp.dot(query_flat, w_query.T, preferred_element_type=jnp.float32)
    grad_input = grad_input + jnp.dot(key_flat, w_key.T, preferred_element_type=jnp.float32)
    grad_input = grad_input + jnp.dot(value_flat, w_value.T, preferred_element_type=jnp.float32)
    weight_grads = (
        jnp.dot(flat_in.T, query_flat, preferred_element_type=jnp.float32),
        jnp.dot(flat_in.T, key_flat, preferred_element_type=jnp.float32),
        jnp.dot(flat_in.T, value_flat, preferred_element_type=jnp.float32),
    )
    return (grad_input.reshape(inputs.shape), weight_grads)


def group_backward(inputs, positions, cotangent, state, projections, dense, route):
    queries, key_rows, value_rows, key_all, value_all, pos_all, attended, log_total, kept = state
    grad_middle, grad_att, dense_grads = dense_backward(cotangent, attended, kept, dense)
    soft_full, grad_score, inner_sum, grad_query = query_grads(
        queries, key_all, value_all, positions, pos_all, log_total, grad_att
    )
    sum_key, sum_value = route(
        queries,
        grad_att,
        soft_full,
        grad_score,
        log_total,
        inner_sum,
        positions,
        key_rows,
        value_rows,
    )
    grad_key = sum_key.astype(jnp.bfloat16)
    grad_value = sum_value.astype(jnp.bfloat16)
    grad_input, weight_grads = input_grads(
        inputs, grad_middle, grad_query, grad_key, grad_value, projections
    )
    return (grad_input, weight_grads + dense_grads)


def per_device(
    x_short,
    order_short,
    x_long,
    order_long,
    w_query,
    w_key,
    w_value,
    w_out,
    b_out,
    alphas,
    w_up,
    b_up,
    w_down,
    b_down,
    cot_short,
    cot_long,
):
    projections = (w_query, w_key, w_value)
    dense = (w_out, b_out, alphas, w_up, b_up, w_down, b_down)
    query_s = project(x_short, w_query)
    key_s = project(x_short, w_key)
    value_s = project(x_short, w_value)
    key_all_s, value_all_s, pos_all_s = (
        lax.all_gather(key_s, "seq", axis=1, tiled=True),
        lax.all_gather(value_s, "seq", axis=1, tiled=True),
        lax.all_gather(order_short, "seq", axis=0, tiled=True),
    )
    query_l = project(x_long, w_query)
    key_l = project(x_long, w_key)
    value_l = project(x_long, w_value)
    key_all_l, value_all_l, pos_all_l = (
        lax.all_gather(key_l, "seq", axis=1, tiled=True),
        lax.all_gather(value_l, "seq", axis=1, tiled=True),
        lax.all_gather(order_long, "seq", axis=0, tiled=True),
    )
    att_s, lse_s = attend(query_s, key_all_s, value_all_s, order_short, pos_all_s)
    kept_s = dense_forward(x_short, att_s, dense)
    att_l, lse_l = attend(query_l, key_all_l, value_all_l, order_long, pos_all_l)
    kept_l = dense_forward(x_long, att_l, dense)
    out_short = kept_s[-1].reshape(x_short.shape).astype(jnp.bfloat16)
    out_long = kept_l[-1].reshape(x_long.shape).astype(jnp.bfloat16)

    def route_short(
        queries,
        grad_att,
        soft_full,
        grad_score,
        log_total,
        inner_sum,
        positions,
        key_rows,
        value_rows,
    ):
        part_key, part_value = key_partials(queries, grad_att, soft_full, grad_score)
        return (
            lax.psum_scatter(part_key, "seq", scatter_dimension=1, tiled=True),
            lax.psum_scatter(part_value, "seq", scatter_dimension=1, tiled=True),
        )

    def route_long(
        queries,
        grad_att,
        soft_full,
        grad_score,
        log_total,
        inner_sum,
        positions,
        key_rows,
        value_rows,
    ):
        part_key, part_value = key_partials(queries, grad_att, soft_full, grad_score)
        return (
            lax.psum_scatter(part_key, "seq", scatter_dimension=1, tiled=True),
            lax.psum_scatter(part_value, "seq", scatter_dimension=1, tiled=True),
        )

    state_s = (query_s, key_s, value_s, key_all_s, value_all_s, pos_all_s, att_s, lse_s, kept_s)
    dx_short, grads_s = group_backward(
        x_short, order_short, cot_short, state_s, projections, dense, route_short
    )
    state_l = (query_l, key_l, value_l, key_all_l, value_all_l, pos_all_l, att_l, lse_l, kept_l)
    dx_long, grads_l = group_backward(
        x_long, order_long, cot_long, state_l, projections, dense, route_long
    )
    local_sums = jax.tree.map(jnp.add, grads_s, grads_l)
    (
        sum_query,
        sum_key,
        sum_value,
        sum_out,
        sum_bout,
        sum_alphas,
        sum_up,
        sum_bup,
        sum_down,
        sum_bdown,
    ) = local_sums
    g_query, g_key, g_value, g_out, g_bout, g_alphas, g_up, g_bup, g_down, g_bdown = lax.psum(
        (
            sum_query,
            sum_key,
            sum_value,
            sum_out,
            sum_bout,
            sum_alphas,
            sum_up,
            sum_bup,
            sum_down,
            sum_bdown,
        ),
        ("dp", "seq"),
    )
    return (
        out_short,
        out_long,
        dx_short,
        dx_long,
        g_query,
        g_key,
        g_value,
        g_out,
        g_bout,
        g_alphas,
        g_up,
        g_bup,
        g_down,
        g_bdown,
    )


def solution(mesh):
    placed = (
        P("dp", "seq", None),
        P("seq"),
        P("dp", "seq", None),
        P("seq"),
        P(),
        P(),
        P(),
        P(),
        P(),
        P(),
        P(),
        P(),
        P(),
        P(),
        P("dp", "seq", None),
        P("dp", "seq", None),
    )
    return jax.shard_map(
        per_device,
        mesh=mesh,
        in_specs=placed,
        out_specs=(
            P("dp", "seq", None),
            P("dp", "seq", None),
            P("dp", "seq", None),
            P("dp", "seq", None),
            P(),
            P(),
            P(),
            P(),
            P(),
            P(),
            P(),
            P(),
            P(),
            P(),
        ),
        check_vma=False,
    )
```

profile of v0, /device:TPU:0, one launch (start us, length us, event | category | flops | bytes accessed | tf_op | source)
XLA Modules:
  0.0 782.6 jit_solution(5360356151151838100)
XLA Ops:
  7.3 2.3 convolution_convert_fusion.5
  11.8 2.7 convolution_convert_fusion.1
  14.7 2.5 convolution_convert_fusion.3
  21.0 12.7 %all-gather = s32[4,1,128]{2,1,0:T(1,128)S(1)} all-gather(s32[1,1,128]{2,1,0:T(1,128)S(1)} %bitcast.250), channel_id=1, replica_groups=mesh['dp'=8,'seq'=4] {'seq'}, dimensions={0}, use_global_device_ids=true | all-gather | bytes 2560 | tf_op jit(solution)/shard_map/all_gather | solution.py:199
  34.4 6.5 all-gather.9.cloned.1.call-done
  40.9 2.3 copy.78
  43.2 27.3 %all-gather.7.cloned.1.call-done = bf16[2,512,512]{2,1,0:T(8,128)(2,1)} async-done(((bf16[2,128,512]{2,1,0:T(8,128)(2,1)}), bf16[2,512,512]{2,1,0:T(8,128)(2,1)}) %all-gather.7.cloned.1.call-update) | async-done | bytes 1048592 | tf_op jit(solution)/shard_map/all_gather | solution.py:198
  70.5 2.3 copy.76
  81.4 3.5 fusion.44
  84.9 2.4 convert_reduce_fusion.1
  88.3 2.8 convert_reduce_fusion.5
  94.7 4.5 fusion.23
  99.2 2.9 copy.92
  102.5 2.5 convolution_convert_fusion.2
  105.0 3.2 reshape.172
  108.2 2.6 copy.84
  110.9 9.7 %all-gather.1 = s32[4,1,256]{2,1,0:T(1,128)S(1)} all-gather(s32[1,1,256]{2,1,0:T(1,128)S(1)} %bitcast.249), channel_id=1, replica_groups=mesh['dp'=8,'seq'=4] {'seq'}, dimensions={0}, use_global_device_ids=true | all-gather | bytes 5120 | tf_op jit(solution)/shard_map/all_gather | solution.py:207
  120.7 2.8 fusion.28
  123.6 4.2 multiply_reduce_fusion.1
  131.9 2.9 copy.90
  135.0 4.6 copy.83
  139.7 14.7 %fusion.6 = (f32[3,8,256]{2,1,0:T(8,128)S(1)}, f32[3,8,256,1024]{3,2,1,0:T(8,128)}) fusion(pred[256,1024]{1,0:T(8,128)(4,1)S(1)} %broadcast_compare_fusion, bf16[3,256,8,64]{1,3,2,0:T(8,128)(2,1)} %copy.84, bf16[3,1024,8,64]{1,3,2,0:T(8,128)(2,1)} %bitcast.206), kind=kOutput, calls=%fused_computation.11 | convolution fusion | flops 824174592 | bytes 29384704 | tf_op jit(solution)/shard_map/sqhe,skhe->shqk/dot_general | solution.py:21
  154.4 11.6 %fusion = f32[3,8,256]{2,1,0:T(8,128)S(1)} fusion(f32[3,8,256]{2,1,0:T(8,128)S(1)} %get-tuple-element.87, f32[3,8,256,1024]{3,2,1,0:T(8,128)} %get-tuple-element.88, pred[256,1024]{1,0:T(8,128)(4,1)S(1)} %broadcast_compare_fusion), kind=kLoop, calls=%fused_computation.6 | loop fusion | flops 25159680 | bytes 25477120 | tf_op jit(solution)/shard_map/reduce_sum | solution.py:35
  165.9 33.3 %all-gather.11.cloned.1.call-done = bf16[3,1024,512]{2,1,0:T(8,128)(2,1)} async-done(((bf16[3,256,512]{2,1,0:T(8,128)(2,1)}), bf16[3,1024,512]{2,1,0:T(8,128)(2,1)}) %all-gather.11.cloned.1.call-update) | async-done | bytes 3145744 | tf_op jit(solution)/shard_map/all_gather | solution.py:206
  199.3 4.6 copy.81
  203.9 12.9 %fusion.37 = bf16[3,256,8,64]{1,3,2,0:T(8,128)(2,1)S(1)} fusion(bf16[3,1024,8,64]{1,3,2,0:T(8,128)(2,1)} %bitcast.213, f32[3,8,256]{2,1,0:T(8,128)S(1)} %fusion, f32[3,8,256]{2,1,0:T(8,128)S(1)} %get-tuple-element.87, f32[3,8,256,1024]{3,2,1,0:T(8,128)} %get-tuple-element.88, pred[256,1024]{1,0:T(8,128)(4,1)S(1)} %broadcast_compare_fusion), kind=kOutput, calls=%fused_computation.83 | convolution fusion | flops 837156864 | bytes 29409280 | tf_op jit(solution)/shard_map/shqk,skhe->sqhe/dot_general | solution.py:37
  220.0 3.5 multiply_convert_fusion.1
  223.5 5.7 convert_reduce_fusion
  231.1 5.2 fusion.29
  238.6 2.4 reshape.174
  242.7 13.3 %fusion.2 = f32[3,8,64,1024]{3,2,1,0:T(8,128)} fusion(bf16[3,256,8,64]{1,3,2,0:T(8,128)(2,1)} %copy.94, f32[3,8,256]{2,1,0:T(8,128)S(1)} %log_add_fusion, f32[3,8,256,1024]{3,2,1,0:T(8,128)} %get-tuple-element.88, pred[256,1024]{1,0:T(8,128)(4,1)S(1)} %broadcast_compare_fusion), kind=kOutput, calls=%fused_computation.8 | convolution fusion | flops 830472192 | bytes 32530432 | tf_op jit(solution)/shard_map/shqk,sqhe->skhe/dot_general | solution.py:71
  256.0 6.6 copy.99
  263.7 19.4 %multiply_reduce_fusion = (f32[3,8,256]{2,1,0:T(8,128)S(1)}, f32[3,8,256,1024]{3,2,1,0:T(8,128)}) fusion(f32[3,8,256]{2,1,0:T(8,128)S(1)} %log_add_fusion, f32[3,8,256,1024]{3,2,1,0:T(8,128)} %get-tuple-element.88, pred[256,1024]{1,0:T(8,128)(4,1)S(1)} %broadcast_compare_fusion, bf16[3,256,8,64]{1,3,2,0:T(8,128)(2,1)S(1)} %copy-done.36, ...), kind=kOutput, calls=%fused_computation.1 | convolution fusion | flops 836757504 | bytes 54575104 | tf_op jit(solution)/shard_map/sqhe,skhe->shqk/dot_general | solution.py:48
  283.1 18.1 %multiply_convert_fusion = bf16[3,8,256,1024]{3,2,1,0:T(8,128)(2,1)S(1)} fusion(f32[3,8,256,1024]{3,2,1,0:T(8,128)} %get-tuple-element.97, f32[3,8,256]{2,1,0:T(8,128)S(1)} %get-tuple-element.96, f32[3,8,256]{2,1,0:T(8,128)S(1)} %log_add_fusion, f32[3,8,256,1024]{3,2,1,0:T(8,128)} %get-tuple-element.88, pred[256,1024]{1,0:T(8,128)(4,1)S(1)} %broadcast_compare_fusion), kind=kLoop, calls=%fused_computation | loop fusion | flops 37748736 | bytes 63225856 | tf_op jit(solution)/shard_map/convert_element_type | solution.py:55
  301.2 5.8 broadcast_multiply_fusion
  307.7 6.6 copy.97
  319.1 8.5 %fusion.36 = bf16[3,256,8,64]{1,3,2,0:T(8,128)(2,1)S(1)} fusion(bf16[3,1024,8,64]{1,3,2,0:T(8,128)(2,1)S(1)} %bitcast.207, bf16[3,8,256,1024]{3,2,1,0:T(8,128)(2,1)} %copy-done.2), kind=kOutput, calls=%fused_computation.82 | convolution fusion | flops 806092800 | bytes 16515072 | tf_op jit(solution)/shard_map/shqk,skhe->sqhe/dot_general | solution.py:56
  336.1 2.8 convolution_add_fusion.1
  338.8 3.2 convolution_add_fusion
  344.3 57.4 %reduce-scatter.11.cloned.1.call-done = f32[3,256,512]{2,1,0:T(8,128)} async-done(((f32[3,1024,512]{2,1,0:T(8,128)}), f32[3,256,512]{2,1,0:T(8,128)}) %reduce-scatter.11.cloned.1.call-update) | async-done | bytes 1572880 | tf_op jit(solution)/shard_map/reduce_scatter | solution.py:247
  404.9 110.5 %reduce-scatter.9.cloned.1.call-done = f32[3,256,512]{2,1,0:T(8,128)} async-done(((f32[3,1024,512]{2,1,0:T(8,128)}), f32[3,256,512]{2,1,0:T(8,128)}) %reduce-scatter.9.cloned.1.call-update) | async-done | bytes 1572880 | tf_op jit(solution)/shard_map/reduce_scatter | solution.py:246
  523.3 2.3 convolution_add_fusion.10
  525.7 2.5 maximum_add_fusion
  528.1 42.3 %all-reduce = (f32[512]{0:T(512)}, f32[2]{0:T(128)}, f32[2048]{0:T(1024)}, f32[512]{0:T(512)}) all-reduce(f32[512]{0:T(512)S(1)} %add.222, f32[2]{0:T(128)S(1)} %maximum_add_fusion, f32[2048]{0:T(1024)S(1)} %add.225, f32[512]{0:T(512)S(1)} %add.227), channel_id=1, replica_groups=mesh['dp'=8,'seq'=4] {'dp','seq'}, use_global_device_ids=true, to_apply=%region_16.17 | all-reduce | flops 3074 | bytes 24592 | tf_op jit(solution)/shard_map/psum | solution.py:271
  576.5 184.8 %all-reduce.4.cloned.1.call-done = (f32[512,512]{0,1:T(8,128)}, f32[512,512]{0,1:T(8,128)}, f32[512,512]{0,1:T(8,128)}, f32[512,512]{1,0:T(8,128)}, f32[512,2048]{1,0:T(8,128)}, /*index=5*/f32[2048,512]{1,0:T(8,128)}) async-done(((f32[512,512]{0,1:T(8,128)}, f32[512,512]{0,1:T(8,128)}, f32[512,512]{0,1:T(8,128)}, f32[512,512]{1,0:T(8,128)}, f32[512,2048]{1,0:T(8,128)}, /*index=5*/f32[2048,512]{1,0:T(8,128)}), ...) | async-done | bytes 12582928 | tf_op jit(solution)/shard_map/psum | solution.py:271
  761.2 2.7 copy.104
  763.9 2.5 copy.105
  768.7 4.8 copy.148
  (222 shorter events, 72.0 us)
Async XLA Ops:
  7.2 73.4 %copy-start = (bf16[512,2048]{1,0:T(8,128)(2,1)S(1)}, bf16[512,2048]{1,0:T(8,128)(2,1)}, u32[]{:S(2)}) copy-start(bf16[512,2048]{1,0:T(8,128)(2,1)} %param.26) | copy-start | bytes 6291460
  7.2 7.5 copy-start.10
  7.2 33.7 %all-gather.9.cloned.1.call-start = ((), (), s32[]{:S(2)}) async-start(), calls=%async_computation.5 | async-start | bytes 1310720 | tf_op jit(solution)/shard_map/all_gather | solution.py:197
  9.6 60.9 %all-gather.7.cloned.1.call-start = ((), (), s32[]{:S(2)}) async-start(), calls=%async_computation.4 | async-start | bytes 1310720 | tf_op jit(solution)/shard_map/all_gather | solution.py:198
  11.8 5.5 copy-start.8
  11.8 123.2 %all-gather.13.cloned.1.call-start = ((), (), s32[]{:S(2)}) async-start(), calls=%async_computation.7 | async-start | bytes 3932160 | tf_op jit(solution)/shard_map/all_gather | solution.py:205
  14.6 6.4 copy-start.65
  14.6 19.1 %copy-start.66 = (f32[2]{0:T(128)S(1)}, f32[2]{0:T(128)}, u32[]{:S(2)}) copy-start(f32[2]{0:T(128)} %param.25) | copy-start | bytes 28
  14.6 184.6 %all-gather.11.cloned.1.call-start = ((), (), s32[]{:S(2)}) async-start(), calls=%async_computation.6 | async-start | bytes 3932160 | tf_op jit(solution)/shard_map/all_gather | solution.py:206
  17.2 324.9 %reduce-scatter.7.cloned.1.call-start = ((), (), s32[]{:S(2)}) async-start(), calls=%async_computation.9 | async-start | bytes 2621440 | tf_op jit(solution)/shard_map/reduce_scatter | solution.py:230
  74.9 3.5 copy-start.3
  76.9 3.7 copy-start.60
  81.4 3.6 copy-start.13
  94.6 4.6 copy-start.42
  102.1 8.7 %copy-start.64 = (s32[256]{0:T(256)S(1)}, s32[256]{0:T(256)}, u32[]{:S(2)}) copy-start(s32[256]{0:T(256)} %param.19) | copy-start | bytes 3076
  102.1 241.0 %reduce-scatter.5.cloned.1.call-start = ((), (), s32[]{:S(2)}) async-start(), calls=%async_computation.8 | async-start | bytes 2621440 | tf_op jit(solution)/shard_map/reduce_scatter | solution.py:229
  123.6 4.2 copy-start.4
  134.8 267.0 %reduce-scatter.11.cloned.1.call-start = ((), (), s32[]{:S(2)}) async-start(), calls=%async_computation.11 | async-start | bytes 7864320 | tf_op jit(solution)/shard_map/reduce_scatter | solution.py:247
  219.9 3.5 copy-start.22
  219.9 3.5 copy-start.56
  219.9 3.5 copy-start.68
  223.5 7.6 copy-start.70
  223.5 5.7 copy-start.34
  231.0 5.2 copy-start.49
  262.6 252.8 %reduce-scatter.9.cloned.1.call-start = ((), (), s32[]{:S(2)}) async-start(), calls=%async_computation.10 | async-start | bytes 7864320 | tf_op jit(solution)/shard_map/reduce_scatter | solution.py:246
  283.1 18.2 %copy-start.15 = (bf16[3,256,8,64]{1,3,2,0:T(8,128)(2,1)S(1)}, bf16[3,256,8,64]{1,3,2,0:T(8,128)(2,1)}, u32[]{:S(2)}) copy-start(bf16[3,256,8,64]{1,3,2,0:T(8,128)(2,1)} %copy.84) | copy-start | bytes 2359300
  301.2 6.5 copy-start.2
  314.3 4.1 copy-start.44
  314.3 4.4 copy-start.9
  314.4 446.9 %all-reduce.4.cloned.1.call-start = ((), (), s32[]{:S(2)}) async-start(), calls=%async_computation.12 | async-start | bytes 25165824 | tf_op jit(solution)/shard_map/psum | solution.py:271
  315.9 3.2 copy-start.5
  329.0 3.1 copy-start.57
  329.0 3.1 copy-start.71
  343.1 174.5 %copy-start.39 = (bf16[2,128,512]{2,1,0:T(8,128)(2,1)}, bf16[2,128,512]{2,1,0:T(8,128)(2,1)S(1)}, u32[]{:S(2)}) copy-start(bf16[2,128,512]{2,1,0:T(8,128)(2,1)S(1)} %convert_element_type.203) | copy-start | bytes 786436
  344.3 174.6 %copy-start.41 = (bf16[2,128,512]{2,1,0:T(8,128)(2,1)}, bf16[2,128,512]{2,1,0:T(8,128)(2,1)S(1)}, u32[]{:S(2)}) copy-start(bf16[2,128,512]{2,1,0:T(8,128)(2,1)S(1)} %convert_element_type.201) | copy-start | bytes 786436
  517.0 3.5 copy-start.20
  520.5 5.1 copy-start.63
  520.5 5.1 copy-start.62
  520.6 49.9 %copy-start.17 = (bf16[64,8,3,256]{3,1,2,0:T(8,128)(2,1)S(1)}, bf16[64,8,3,256]{3,1,2,0:T(8,128)(2,1)}, u32[]{:S(2)}) copy-start(bf16[64,8,3,256]{3,1,2,0:T(8,128)(2,1)} %copy-done.16) | copy-start | bytes 2359300
  520.6 50.5 %copy-start.27 = (bf16[512,512]{1,0:T(8,128)(2,1)S(1)}, bf16[512,512]{1,0:T(8,128)(2,1)}, u32[]{:S(2)}) copy-start(bf16[512,512]{1,0:T(8,128)(2,1)} %param.21) | copy-start | bytes 1572868
  523.3 49.6 %copy-start.28 = (bf16[512,512]{1,0:T(8,128)(2,1)S(1)}, bf16[512,512]{1,0:T(8,128)(2,1)}, u32[]{:S(2)}) copy-start(bf16[512,512]{1,0:T(8,128)(2,1)} %param.22) | copy-start | bytes 1572868
  523.3 49.6 %copy-start.40 = (bf16[2,128,512]{2,1,0:T(8,128)(2,1)S(1)}, bf16[2,128,512]{2,1,0:T(8,128)(2,1)}, u32[]{:S(2)}) copy-start(bf16[2,128,512]{2,1,0:T(8,128)(2,1)} %copy-done.39) | copy-start | bytes 786436
  570.5 3.6 copy-start.21
  571.5 3.2 copy-start.50
  761.2 5.2 copy-start.53
  761.2 6.5 copy-start.52
  768.7 4.9 copy-start.32
  768.7 6.9 copy-start.1
  (33 other events, 60.7 us)
Sparse Core Ops, SparseCore 0:
  10.2 30.6 all-gather.8
  43.0 27.4 all-gather.6
  72.1 62.9 all-gather.12
  137.0 62.1 all-gather.10
  201.4 42.5 reduce-scatter.6
  246.2 43.1 reduce-scatter.4
  291.8 109.9 reduce-scatter.10
  404.1 111.2 reduce-scatter.8
  523.0 238.2 all-reduce.3
where the time goes:
time: 793 us; the launch traced here: 783 us
  waiting for transfers between devices  420 us (53%)
  matrix products  160 us (20%)
  local copies, waits for them, and re-layouts  75.7 us (10%)
  blocking collectives  64.7 us (8%)
  other arithmetic  45.5 us (6%)
  between operations  15.3 us (2%)
    psum x1, waiting for transfers between devices, per_device(): lax.psum((sum_query, sum_key, sum_value, sum_out, sum_bout, sum_alphas, s...  185 us
    reduce_scatter x1, waiting for transfers between devices, route_long(): lax.psum_scatter(part_key, 'seq', scatter_dimension=1, tiled=True)  111 us
    reduce_scatter x1, waiting for transfers between devices, route_long(): lax.psum_scatter(part_value, 'seq', scatter_dimension=1, tiled=True)  57.4 us
    psum x1, blocking collectives, per_device(): lax.psum((sum_query, sum_key, sum_value, sum_out, sum_bout, sum_alphas, s...  42.3 us
    all_gather x1, waiting for transfers between devices, per_device(): lax.all_gather(value_l, 'seq', axis=1, tiled=True)  33.3 us
    all_gather x1, waiting for transfers between devices, per_device(): lax.all_gather(value_s, 'seq', axis=1, tiled=True)  27.3 us
    unnamed x152, local copies, waits for them, and re-layouts  25.7 us
    dot_general x2, matrix products, query_grads(): jnp.einsum('sqhe,skhe->shqk', heads_view(grad_att), heads_view(value_all)...  23.6 us
  transfers between devices with their start and end apart: 9, of which 7 were waited for; matrix products, arithmetic and copies ran while one was open for 32% of the time, Pallas kernels for 0%

commit v1 on v0

v1 whole, which is shorter than its diff:
```python
import functools
import jax
import jax.numpy as jnp
from jax import lax
from jax.sharding import PartitionSpec as P
from jax.experimental import pallas as pl
from jax.experimental.pallas import tpu as pltpu

BF = jnp.bfloat16
F32 = jnp.float32
HEADS = 8
HD = 64
D = 512
FF = 2048
T = 1024
SUB = 64
NSUB = T // SUB
QB = 256
NQ = T // QB


def dot(a, b, ca=1, cb=0):
    return lax.dot_general(a, b, (((ca,), (cb,)), ((), ())), preferred_element_type=F32)


def params(mb):
    return pltpu.CompilerParams(vmem_limit_bytes=mb * 1024 * 1024)


def attn_fwd_body(dst, bias, c0, c1, c2, c3, mask, w, wt, xs, qh, kh, vh, qt, kt, vt, ot, att, lse, sem):
    copies = []
    for s in range(NSUB):
        src = (c0, c1, c2, c3)[s // 4].at[pl.ds((s % 4) * SUB, SUB)]
        copies.append(pltpu.make_async_copy(src, xs.at[pl.ds(pl.multiple_of(dst[s] * SUB, SUB), SUB)], sem.at[s]))
    for c in copies:
        c.start()
    for c in copies:
        c.wait()

    def proj(i, carry):
        rows = pl.ds(pl.multiple_of(i * QB, QB), QB)
        x = xs[rows, :]
        qkv = dot(x, w[...]).astype(BF)
        qkvt = dot(wt[...], x, 1, 1).astype(BF)
        for h in range(HEADS):
            qh[h, rows, :] = qkv[:, h * HD:(h + 1) * HD] * BF(0.125)
            kh[h, rows, :] = qkv[:, D + h * HD:D + (h + 1) * HD]
            vh[h, rows, :] = qkv[:, 2 * D + h * HD:2 * D + (h + 1) * HD]
        qt[:, rows] = qkvt[:D] * BF(0.125)
        kt[:, rows] = qkvt[D:2 * D]
        vt[:, rows] = qkvt[2 * D:]
        return carry

    lax.fori_loop(0, NQ, proj, 0)

    def head(h, carry):
        hr = pl.ds(pl.multiple_of(h * HD, HD), HD)
        for i in range(NQ):
            cols = pl.ds(i * QB, QB)
            q = qt[hr, cols]
            tiles, tops = [], []
            for j in range(i + 1):
                s = dot(kh[h, pl.ds(j * QB, QB), :], q)
                if j == i:
                    s = s + mask[i]
                    tops.append(jnp.max(s, axis=0, keepdims=True))
                else:
                    tops.append(jnp.max(s, axis=0, keepdims=True) + bias[i * NQ + j])
                tiles.append(s)
            m = functools.reduce(jnp.maximum, tops)
            total, o = None, None
            for j in range(i + 1):
                mj = m if j == i else m - bias[i * NQ + j]
                e = jnp.exp(tiles[j] - mj)
                t = jnp.sum(e, axis=0, keepdims=True)
                total = t if total is None else total + t
                p = dot(vt[hr, pl.ds(j * QB, QB)], e.astype(BF))
                o = p if o is None else o + p
            o = o * (1.0 / total)
            ot[hr, cols] = o
            lse[h, :, cols] = m + jnp.log(total)
        return carry

    lax.fori_loop(0, HEADS, head, 0)
    for i in range(NQ):
        rows = pl.ds(i * QB, QB)
        att[rows, :] = ot[:, rows].T.astype(BF)


def attn_fwd(dst, bias, chunks, mask, w, wt):
    s = jax.ShapeDtypeStruct
    hb = s((HEADS, T, HD), BF)
    tb = s((D, T), BF)
    anyspec = pl.BlockSpec(memory_space=pl.ANY)
    smem = pl.BlockSpec(memory_space=pltpu.SMEM)
    vmem = pl.BlockSpec(memory_space=pltpu.VMEM)
    return pl.pallas_call(
        attn_fwd_body,
        out_shape=(s((T, D), BF), hb, hb, hb, tb, tb, tb, s((D, T), F32), s((T, D), BF), s((HEADS, 1, T), F32)),
        in_specs=[smem, smem] + [anyspec] * 4 + [vmem] * 3,
        out_specs=(vmem,) * 10,
        scratch_shapes=[pltpu.SemaphoreType.DMA((NSUB,))],
        compiler_params=params(40),
        cost_estimate=pl.CostEstimate(flops=12_000_000_000, bytes_accessed=16_000_000, transcendentals=5_000_000),
        name="attn_fwd",
    )(dst, bias, *chunks, mask, w, wt)


FB = 256
NF = FF // FB
SLOTS = 32
R1 = 304
R2 = 96


def scatter_rows(dst, rows_ref, outs, sem):
    copies = []
    for s in range(NSUB):
        to = outs[s // 4].at[pl.ds((s % 4) * SUB, SUB)]
        copies.append(pltpu.make_async_copy(rows_ref.at[pl.ds(pl.multiple_of(dst[s] * SUB, SUB), SUB)], to, sem.at[s]))
    for c in copies:
        c.start()
    return copies


def gather_rows(dst, ins, rows_ref, sem):
    copies = []
    for s in range(NSUB):
        src = ins[s // 4].at[pl.ds((s % 4) * SUB, SUB)]
        copies.append(pltpu.make_async_copy(src, rows_ref.at[pl.ds(pl.multiple_of(dst[s] * SUB, SUB), SUB)], sem.at[s]))
    for c in copies:
        c.start()
    return copies


def put_slot(me, keep, send, part, s, row, rows, val):
    slot = jnp.bitwise_xor(s, me[part])
    at = pl.ds(row, rows)

    @pl.when(slot < SLOTS // 2)
    def _():
        keep[part, slot, at, :] = val

    @pl.when(slot >= SLOTS // 2)
    def _():
        send[part, slot - SLOTS // 2, at, :] = val


def top_row(vals):
    rows = lax.broadcasted_iota(jnp.int32, (16, 128), 0)
    return jnp.where(rows == 0, jnp.broadcast_to(vals, (16, 128)), 0.0).astype(BF)


def ffn_body(n_dev, dst, me, alphas, c0, c1, c2, c3, xs, att, ot, w_out, b_out, w_up, b_up, w_down, b_down,
             o0, o1, o2, o3, gm_out, doh, dott, inner, keep, send,
             cot, branch, middle, low, gfeed, feed, gm, out_rows, sem, sem2):
    f = pl.program_id(0)
    a0, a1 = alphas[0], alphas[1]

    @pl.when(f == 0)
    def _():
        copies = gather_rows(dst, (c0, c1, c2, c3), cot, sem)
        br = dot(att[...], w_out[...]) + b_out[...]
        branch[...] = br
        mid = xs[...].astype(F32) + a0 * br
        middle[...] = mid
        low[...] = mid.astype(BF)
        for c in copies:
            c.wait()
        g = cot[...].astype(F32)
        gfeed[...] = (a1 * g).astype(BF)
        gm[...] = g
        feed[...] = jnp.broadcast_to(b_down[...], feed.shape)

    hidden = dot(low[...], w_up[...]) + b_up[...]
    c = 0.7978845608028654
    h2 = hidden * hidden
    th = jnp.tanh(hidden * (c + (c * 0.044715) * h2))
    half = 0.5 + 0.5 * th
    active = (hidden * half).astype(BF)
    slope = half + (0.5 * hidden) * (1.0 - th * th) * (c + (3 * c * 0.044715) * h2)
    feed[...] += dot(active, w_down[...])
    grad_h = (dot(gfeed[...], w_down[...], 1, 1) * slope).astype(BF)
    bu = jnp.sum(grad_h.astype(F32), axis=0, keepdims=True)
    gd = dot(active, gfeed[...], 0, 0)
    gu = dot(low[...], grad_h, 0, 0)
    gm[...] += dot(grad_h, w_up[...], 1, 1)
    for b in range(2):
        for a in range(2):
            put_slot(me, keep, send, 0, 4 * f + 2 * b + a, 0, 256,
                     gu[a * 256:(a + 1) * 256, b * 128:(b + 1) * 128].astype(BF))
        put_slot(me, keep, send, 0, 2 * f + b, 288, 16, top_row(bu[:, b * 128:(b + 1) * 128]))
    for lb in range(4):
        put_slot(me, keep, send, 1, lb * 8 + f, 0, 256, gd[:, lb * 128:(lb + 1) * 128].astype(BF))

    @pl.when(f == NF - 1)
    def _():
        out_rows[...] = (middle[...] + a1 * feed[...]).astype(BF)
        copies = scatter_rows(dst, out_rows, (o0, o1, o2, o3), sem2)
        g = cot[...].astype(F32)
        s1 = jnp.sum(feed[...] * g)
        s0 = jnp.sum(branch[...] * gm[...])
        bd = jnp.sum(gfeed[...].astype(F32), axis=0, keepdims=True)
        gm_out[...] = gm[...]
        gb = (a0 * gm[...]).astype(BF)
        bo = jnp.sum(gb.astype(F32), axis=0, keepdims=True)
        go = dot(att[...], gb, 0, 0)
        da = dot(gb, w_out[...], 1, 1).astype(BF)
        for h in range(HEADS):
            doh[h] = da[:, h * HD:(h + 1) * HD]
        dt = dot(w_out[...], gb, 1, 1).astype(BF)
        dott[...] = dt
        for h in range(HEADS):
            hs = slice(h * HD, (h + 1) * HD)
            inner[h] = jnp.sum(ot[hs, :] * dt[hs, :].astype(F32), axis=0, keepdims=True)
        for s in range(SLOTS):
            lb, a = s // 8, s % 8
            for part in range(2):
                r0 = a * 64 + part * 32
                put_slot(me, keep, send, part, s, 256, 32, go[r0:r0 + 32, lb * 128:(lb + 1) * 128].astype(BF))
        for b in range(4):
            put_slot(me, keep, send, 0, 16 + b, 288, 16, top_row(bd[:, b * 128:(b + 1) * 128]))
            put_slot(me, keep, send, 0, 20 + b, 288, 16, top_row(bo[:, b * 128:(b + 1) * 128]))
        zero = jnp.zeros((16, 128), BF)
        for s in range(24, SLOTS):
            put_slot(me, keep, send, 0, s, 288, 16, zero)
        nr = (n_dev + 127) // 128
        row = lax.broadcasted_iota(jnp.int32, (SLOTS, 128), 0)
        lane = lax.broadcasted_iota(jnp.int32, (SLOTS, 128), 1)
        mine_row, mine_lane = me[2] // 128, me[2] % 128
        small = jnp.zeros((SLOTS, 128), F32)
        for k, total in enumerate((s0, s1)):
            rest = jnp.full((SLOTS, 128), total, F32)
            for t in range(3):
                piece = rest.astype(BF).astype(F32)
                rest = rest - piece
                here = (row == (3 * k + t) * nr + mine_row) & (lane == mine_lane)
                small = jnp.where(here, piece, small)
        for s in range(SLOTS):
            put_slot(me, keep, send, 1, s, 288, 16, top_row(small[s:s + 1]))
        for c in copies:
            c.wait()


def ffn(n_dev, dst, me, alphas, cots, xs, att, ot, w_out, b_out, w_up, b_up, w_down, b_down):
    s = jax.ShapeDtypeStruct
    anyspec = pl.BlockSpec(memory_space=pl.ANY)
    smem = pl.BlockSpec(memory_space=pltpu.SMEM)
    vmem = pl.BlockSpec(memory_space=pltpu.VMEM)
    v = pltpu.VMEM
    half = s((2, SLOTS // 2, R1, 128), BF)
    return pl.pallas_call(
        functools.partial(ffn_body, n_dev),
        grid=(NF,),
        out_shape=(s((256, D), BF),) * 4 + (s((T, D), F32), s((HEADS, T, HD), BF), s((D, T), BF),
                                            s((HEADS, 1, T), F32), half, half),
        in_specs=[smem, smem, smem] + [anyspec] * 4 + [vmem] * 5 + [
            pl.BlockSpec((D, FB), lambda f: (0, f)),
            pl.BlockSpec((1, FB), lambda f: (0, f)),
            pl.BlockSpec((FB, D), lambda f: (f, 0)),
            vmem,
        ],
        out_specs=(anyspec,) * 4 + (vmem,) * 6,
        scratch_shapes=[v((T, D), BF), v((T, D), F32), v((T, D), F32), v((T, D), BF), v((T, D), BF), v((T, D), F32),
                        v((T, D), F32), v((T, D), BF), pltpu.SemaphoreType.DMA((NSUB,)), pltpu.SemaphoreType.DMA((NSUB,))],
        compiler_params=params(56),
        cost_estimate=pl.CostEstimate(flops=15_000_000_000, bytes_accessed=20_000_000, transcendentals=2_000_000),
        name="ffn",
    )(dst, me, alphas, *cots, xs, att, ot, w_out, b_out, w_up, b_up, w_down, b_down)


def attn_bwd_body(dst, me, bias, mask, xs, gm, qh, kh, vh, qt, kt, doh, dott, lse, inner, w,
                  d0, d1, d2, d3, keep, send, grads, dx_rows, sem):
    def pair(hp, carry):
        dq2, dk2, dv2 = [], [], []
        for sub in range(2):
            h = hp * 2 + sub
            hr = pl.ds(pl.multiple_of(h * HD, HD), HD)
            dk = [None] * NQ
            dv = [None] * NQ
            dq = []
            for i in range(NQ):
                cols = pl.ds(i * QB, QB)
                q, do = qt[hr, cols], dott[hr, cols]
                q_rows, do_rows = qh[h, cols, :], doh[h, cols, :]
                ls, inn = lse[h, :, cols], inner[h, :, cols]
                acc = None
                for j in range(i + 1):
                    rows = pl.ds(j * QB, QB)
                    s = dot(kh[h, rows, :], q)
                    if j == i:
                        p = jnp.exp(s + mask[i] - ls)
                    else:
                        p = jnp.exp(s - (ls - bias[i * NQ + j]))
                    dp = dot(vh[h, rows, :], do)
                    ds = (p * (dp - inn)).astype(BF)
                    gv = dot(p.astype(BF), do_rows)
                    gk = dot(ds, q_rows)
                    gq = dot(kt[hr, rows], ds)
                    dv[j] = gv if dv[j] is None else dv[j] + gv
                    dk[j] = gk if dk[j] is None else dk[j] + gk
                    acc = gq if acc is None else acc + gq
                dq.append((acc * 0.125).T.astype(BF))
            dq2.append(jnp.concatenate(dq, axis=0))
            dk2.append(jnp.concatenate(dk, axis=0).astype(BF))
            dv2.append(jnp.concatenate(dv, axis=0).astype(BF))
        for n, two in enumerate((dq2, dk2, dv2)):
            lanes = pl.ds(pl.multiple_of(n * D + hp * 128, 128), 128)
            grads[:, lanes] = jnp.concatenate(two, axis=1)
        return carry

    lax.fori_loop(0, HEADS // 2, pair, 0)
    dx_rows[...] = (gm[...] + dot(grads[...], w[...], 1, 1)).astype(BF)
    copies = scatter_rows(dst, dx_rows, (d0, d1, d2, d3), sem)
    for n in range(3):
        g = dot(xs[...], grads[:, n * D:(n + 1) * D], 0, 0)
        for s in range(SLOTS):
            lb, a = s // 8, s % 8
            for part in range(2):
                r0 = a * 64 + part * 32
                put_slot(me, keep, send, part, s, n * 32, 32, g[r0:r0 + 32, lb * 128:(lb + 1) * 128].astype(BF))
    for c in copies:
        c.wait()


def attn_bwd(dst, me, bias, mask, xs, gm, qh, kh, vh, qt, kt, doh, dott, lse, inner, w):
    s = jax.ShapeDtypeStruct
    anyspec = pl.BlockSpec(memory_space=pl.ANY)
    smem = pl.BlockSpec(memory_space=pltpu.SMEM)
    vmem = pl.BlockSpec(memory_space=pltpu.VMEM)
    half = s((2, SLOTS // 2, R2, 128), BF)
    return pl.pallas_call(
        attn_bwd_body,
        out_shape=(s((256, D), BF),) * 4 + (half, half),
        in_specs=[smem] * 3 + [vmem] * 13,
        out_specs=(anyspec,) * 4 + (vmem,) * 2,
        scratch_shapes=[pltpu.VMEM((T, 3 * D), BF), pltpu.VMEM((T, D), BF), pltpu.SemaphoreType.DMA((NSUB,))],
        compiler_params=params(56),
        cost_estimate=pl.CostEstimate(flops=18_000_000_000, bytes_accessed=20_000_000, transcendentals=5_000_000),
        name="attn_bwd",
    )(dst, me, bias, mask, xs, gm, qh, kh, vh, qt, kt, doh, dott, lse, inner, w)


def pick_half(slot, own, other):
    return jnp.where(slot < SLOTS // 2, own[0, 0].astype(F32), other[0, 0].astype(F32))


def finish_dense_body(slots, own_a, other_a, own_b, other_b, up, down, out, small):
    s = pl.program_id(0)
    a = pick_half(slots[0, s], own_a, other_a)
    b = pick_half(slots[1, s], own_b, other_b)
    up[...] = a[:256]
    down[...] = b[:256]
    out[0:32] = a[256:288]
    out[32:64] = b[256:288]
    small[0, 0:8] = a[288:296]
    small[0, 8:16] = b[288:296]


def finish_qkv_body(slots, own_a, other_a, own_b, other_b, gq, gk, gv):
    s = pl.program_id(0)
    a = pick_half(slots[0, s], own_a, other_a)
    b = pick_half(slots[1, s], own_b, other_b)
    for n, g in enumerate((gq, gk, gv)):
        g[0:32] = a[n * 32:n * 32 + 32]
        g[32:64] = b[n * 32:n * 32 + 32]


def finish(body, slots, own, other, rows, out_shape, out_specs, name):
    def block(part):
        return pl.BlockSpec((1, 1, rows, 128), lambda s, slots: (part, slots[part, s] % (SLOTS // 2), 0, 0))

    return pl.pallas_call(
        body,
        grid_spec=pltpu.PrefetchScalarGridSpec(
            num_scalar_prefetch=1,
            grid=(SLOTS,),
            in_specs=[block(0), block(0), block(1), block(1)],
            out_specs=out_specs,
        ),
        out_shape=out_shape,
        compiler_params=params(16),
        name=name,
    )(slots, own, other, own, other)


def pairs(size, bit):
    return [(a, a ^ bit) for a in range(size)]


def add(a, b):
    return (a.astype(F32) + b.astype(F32)).astype(BF)


def sum_shards(n_dp, n_seq, keep, send):
    def dp(v, bit):
        return lax.ppermute(v, "dp", pairs(n_dp, bit))

    def seq(v, bit):
        return lax.ppermute(v, "seq", pairs(n_seq, bit))

    got = dp(send, 1)
    a, b = add(keep[0], got[0]), add(keep[1], got[1])
    ga, gb = dp(a[8:], 2), dp(b[8:], 4)
    a, b = add(a[:8], ga), add(b[:8], gb)
    ga, gb = dp(a[4:], 4), dp(b[4:], 2)
    ab = jnp.stack([add(a[:4], ga), add(b[:4], gb)])
    ab = ab.reshape((2, 2, 2) + ab.shape[2:])
    ab = add(ab[:, :, 0], seq(ab[:, :, 1], 1))
    ab = add(ab[:, 0], seq(ab[:, 1], 2))
    bit = 8
    while bit < n_dp:
        ab = add(ab, dp(ab, bit))
        bit *= 2
    ab = jnp.stack([ab, seq(ab, 2)], axis=1)
    ab = jnp.stack([ab, seq(ab, 1)], axis=2)
    ab = ab.reshape((2, 4) + ab.shape[3:])
    a, b = ab[0], ab[1]
    a, b = jnp.concatenate([a, dp(a, 4)]), jnp.concatenate([b, dp(b, 2)])
    ab = jnp.stack([jnp.concatenate([a, dp(a, 2)]), jnp.concatenate([b, dp(b, 4)])])
    return ab, dp(ab, 1)


def per_device(n_dp, n_seq, x_short, order_short, x_long, order_long, w_query, w_key, w_value, w_out, b_out, alphas,
               w_up, b_up, w_down, b_down, cot_short, cot_long):
    i = lax.axis_index("seq")
    d = lax.axis_index("dp")
    n_dev = n_dp * n_seq

    def exchange(parts):
        got = [lax.dynamic_index_in_dim(parts, i, 0, False)]
        for k in range(1, n_seq):
            mine = lax.dynamic_index_in_dim(parts, jnp.bitwise_xor(i, k), 0, False)
            got.append(lax.ppermute(mine, "seq", pairs(n_seq, k)))
        return got

    def rows_of(short, long):
        return jnp.concatenate([short.reshape(1, 256, D), long])

    def home(got, dtype):
        def chunk(j):
            k = jnp.bitwise_xor(i, j)
            v = jnp.where(k < 2, jnp.where(k == 0, got[0], got[1]), jnp.where(k == 2, got[2], got[3]))
            return v.astype(dtype)
        return chunk(0).reshape(2, 128, D), jnp.stack([chunk(j) for j in range(1, n_seq)])

    def give_back(mine):
        return [mine[0]] + [lax.ppermute(mine[k], "seq", pairs(n_seq, k)) for k in range(1, n_seq)]

    xs = exchange(rows_of(x_short, x_long))
    pos_short = jnp.concatenate([order_short, order_short + 512])
    pos = exchange(jnp.stack([pos_short, order_long, order_long, order_long]).reshape(4, 2, 128))
    cots = exchange(rows_of(cot_short, cot_long))

    is_short = i == 0
    sub = jnp.stack(pos).reshape(NSUB, SUB)
    low = jnp.min(sub, axis=1)
    dst = jnp.where(is_short, low // SUB, 2 * (low // 128) + jnp.arange(NSUB) % 2).astype(jnp.int32)
    place = dst[None, :] == jnp.arange(NSUB)[:, None]
    sorted_pos = jnp.sum(jnp.where(place[:, :, None], sub[None], 0), axis=1).reshape(NQ, QB)
    mask = jnp.where(sorted_pos[:, :, None] <= sorted_pos[:, None, :], 0.0, -1e30).astype(F32)
    group = jnp.arange(NQ) // 2
    bias = jnp.where(is_short & (group[:, None] != group[None, :]), -1e30, 0.0).astype(F32).reshape(-1)
    c, bx, by = d & 1, (d >> 1) & 1, (d >> 2) & 1
    me = jnp.stack([c * 16 + bx * 8 + by * 4 + i, c * 16 + by * 8 + bx * 4 + i, d * n_seq + i]).astype(jnp.int32)
    slots = jnp.bitwise_xor(me[:2, None], jnp.arange(SLOTS, dtype=jnp.int32)[None, :])

    w = jnp.concatenate([w_query, w_key, w_value], axis=1)
    rows, qh, kh, vh, qt, kt, vt, ot, att, lse = attn_fwd(dst, bias, xs, mask, w, w.T)
    o0, o1, o2, o3, gm, doh, dott, inner, keep, send = ffn(
        n_dev, dst, me, alphas, cots, rows, att, ot, w_out, b_out.reshape(1, D), w_up, b_up.reshape(1, FF),
        w_down, b_down.reshape(1, D))
    outs = give_back((o0, o1, o2, o3))
    d0, d1, d2, d3, keep2, send2 = attn_bwd(dst, me, bias, mask, rows, gm, qh, kh, vh, qt, kt, doh, dott, lse, inner, w)
    dxs = give_back((d0, d1, d2, d3))
    out_short, out_long = home(outs, BF)
    dx_short, dx_long = home(dxs, F32)
    own1, other1 = sum_shards(n_dp, n_seq, keep, send)
    own2, other2 = sum_shards(n_dp, n_seq, keep2, send2)

    s = jax.ShapeDtypeStruct
    wide = pl.BlockSpec((64, 128), lambda s, slots: (s % 8, s // 8))
    g_up, g_down, g_out, small = finish(
        finish_dense_body, slots, own1, other1, R1,
        (s((D, FF), F32), s((FF, D), F32), s((D, D), F32), s((SLOTS, 16, 128), F32)),
        (pl.BlockSpec((256, 128), lambda s, slots: (s % 2, s // 2)),
         pl.BlockSpec((256, 128), lambda s, slots: (s % 8, s // 8)),
         wide,
         pl.BlockSpec((1, 16, 128), lambda s, slots: (s, 0, 0))), "finish_dense")
    g_query, g_key, g_value = finish(
        finish_qkv_body, slots, own2, other2, R2, (s((D, D), F32),) * 3, (wide,) * 3, "finish_qkv")
    flat = small[:24, 0].reshape(-1)
    nr = (n_dev + 127) // 128
    g_alphas = jnp.sum(small[:6 * nr, 8].reshape(2, 3 * nr * 128), axis=1)
    return (out_short, out_long, dx_short, dx_long, g_query, g_key, g_value, g_out, flat[2560:3072], g_alphas,
            g_up, flat[:2048], g_down, flat[2048:2560])


def solution(mesh):
    split = P("dp", "seq", None)
    whole = P()
    return jax.shard_map(
        functools.partial(per_device, mesh.shape["dp"], mesh.shape["seq"]),
        mesh=mesh,
        in_specs=(split, P("seq"), split, P("seq")) + (whole,) * 10 + (split, split),
        out_specs=(split,) * 4 + (whole,) * 10,
        check_vma=False,
    )
```

time: 793 us -> 348 us (0.44); the launches traced: 783 us -> 347 us
  waiting for transfers between devices: 420 us -> 129 us
  matrix products: 160 us -> 0 us
  Pallas kernels: 0 us -> 122 us
  local copies, waits for them, and re-layouts: 75.7 us -> 9.24 us
  starting transfers between devices: 0.97 us -> 67.4 us
  blocking collectives: 64.7 us -> 0 us
  other arithmetic: 45.5 us -> 17.3 us
  between operations: 15.3 us -> 1.19 us
    psum x1 -> x0, waiting for transfers between devices: 185 us -> none  [per_device(): lax.psum((sum_query, sum_key, sum_value, sum_out, sum_bout, sum_alphas, s...]
    reduce_scatter x4 -> x0, waiting for transfers between devices: 168 us -> none  [the longest x1 111 us: route_long(): lax.psum_scatter(part_key, 'seq', scatter_dimension=1, tiled=True)]
    dot_general x48 -> x0, matrix products: 160 us -> none  [the longest x2 23.6 us: query_grads(): jnp.einsum('sqhe,skhe->shqk', heads_view(grad_att), heads_view(value_all)...]
    ppermute x0 -> x43, waiting for transfers between devices: none -> 129 us  [the longest x20 42.5 us: dp(): return lax.ppermute(v, 'dp', pairs(n_dp, bit))]
    pallas_call x0 -> x5, Pallas kernels: none -> 122 us  [the longest x1 34.6 us: attn_bwd(): pl.pallas_call(attn_bwd_body, out_shape=(s((256, D), BF),) * 4 + (half, h...]
    ppermute x0 -> x43, starting transfers between devices: none -> 67.4 us  [the longest x20 19.6 us: dp(): return lax.ppermute(v, 'dp', pairs(n_dp, bit))]
    all_gather x4 -> x0, waiting for transfers between devices: 67.3 us -> none  [the longest x1 33.3 us: per_device(): lax.all_gather(value_l, 'seq', axis=1, tiled=True)]
    psum x1 -> x0, blocking collectives: 42.3 us -> none  [per_device(): lax.psum((sum_query, sum_key, sum_value, sum_out, sum_bout, sum_alphas, s...]
  transfers between devices with their start and end apart: 9 -> 43, of which waited for: 7 -> 25; matrix products, arithmetic and copies ran while one was open for 32% -> 4% of each run, Pallas kernels for 0% -> 20%
where the time goes in v1:
time: 348 us; the launch traced here: 347 us
  waiting for transfers between devices  129 us (37%)
  Pallas kernels  122 us (35%)
  starting transfers between devices  67.4 us (19%)
  other arithmetic  17.3 us (5%)
  local copies, waits for them, and re-layouts  9.24 us (3%)
    ppermute x20, waiting for transfers between devices, dp(): return lax.ppermute(v, 'dp', pairs(n_dp, bit))  42.5 us
    ppermute x8, waiting for transfers between devices, seq(): return lax.ppermute(v, 'seq', pairs(n_seq, bit))  40.5 us
    pallas_call x1, Pallas kernels, attn_bwd(): pl.pallas_call(attn_bwd_body, out_shape=(s((256, D), BF),) * 4 + (half, h...  34.6 us
    pallas_call x1, Pallas kernels, ffn(): pl.pallas_call(functools.partial(ffn_body, n_dev), grid=(NF,), out_shape=...  34.4 us
    pallas_call x2, Pallas kernels, finish(): pl.pallas_call(body, grid_spec=pltpu.PrefetchScalarGridSpec(num_scalar_pr...  30.5 us
    ppermute x9, waiting for transfers between devices, exchange(): got.append(lax.ppermute(mine, 'seq', pairs(n_seq, k)))  23.9 us
    pallas_call x1, Pallas kernels, attn_fwd(): pl.pallas_call(attn_fwd_body, out_shape=(s((T, D), BF), hb, hb, hb, tb, t...  22.7 us
    ppermute x6, waiting for transfers between devices, give_back(): lax.ppermute(mine[k], 'seq', pairs(n_seq, k))  22.4 us
  transfers between devices with their start and end apart: 43, of which 25 were waited for; matrix products, arithmetic and copies ran while one was open for 4% of the time, Pallas kernels for 20%

profile of v1, /device:TPU:0, one launch (start us, length us, event | category | flops | bytes accessed | tf_op | source)
XLA Modules:
  0.0 346.7 jit_solution(18402562951921107651)
XLA Ops:
  2.8 5.1 %collective-permute-start.2 = (s32[2,128]{1,0:T(2,128)S(1)}, s32[2,128]{1,0:T(2,128)S(1)}, u32[]{:S(2)}, u32[]{:S(2)}) collective-permute-start(s32[2,128]{1,0:T(2,128)S(1)} %get-tuple-element.113), channel_id=1, source_target_pairs={{0,3},{1,2},{2,1},{3,0},{4,7},{5,6},{6,5},{7,4},{8,11},{9,10},{10,... | collective-permute-start | bytes 3080 | tf_op jit(solution)/shard_map/ppermute | solution.py:434
  8.6 2.5 fusion.17
  11.1 1.4 collective-permute-start.3
  12.5 2.9 collective-permute-start.4
  19.0 3.8 %collective-permute-start.8 = (bf16[256,512]{1,0:T(8,128)(2,1)}, bf16[256,512]{1,0:T(8,128)(2,1)}, u32[]{:S(2)}, u32[]{:S(2)}) collective-permute-start(bf16[256,512]{1,0:T(8,128)(2,1)} %get-tuple-element.90), channel_id=1, source_target_pairs={{0,3},{1,2},{2,1},{3,0},{4,7},{5,6},{6,5},{7,4},{8,11},{9,10},{10,... | collective-permute-start | bytes 786440 | tf_op jit(solution)/shard_map/ppermute | solution.py:434
  23.5 11.6 %collective-permute-done.6.c1 = bf16[256,512]{1,0:T(8,128)(2,1)} collective-permute-done((bf16[256,512]{1,0:T(8,128)(2,1)}, bf16[256,512]{1,0:T(8,128)(2,1)}, u32[]{:S(2)}, u32[]{:S(2)}) %collective-permute-start.6) | collective-permute-done | bytes 262176 | tf_op jit(solution)/shard_map/ppermute | solution.py:434
  35.1 2.9 collective-permute-start.5
  38.0 12.2 %collective-permute-done.7.c2 = bf16[256,512]{1,0:T(8,128)(2,1)} collective-permute-done((bf16[256,512]{1,0:T(8,128)(2,1)}, bf16[256,512]{1,0:T(8,128)(2,1)}, u32[]{:S(2)}, u32[]{:S(2)}) %collective-permute-start.7) | collective-permute-done | bytes 262176 | tf_op jit(solution)/shard_map/ppermute | solution.py:434
  50.2 22.7 %attn_fwd.1 = (bf16[1024,512]{1,0:T(8,128)(2,1)S(1)}, bf16[8,1024,64]{2,1,0:T(8,128)(2,1)S(1)}, bf16[8,1024,64]{2,1,0:T(8,128)(2,1)}, bf16[8,1024,64]{2,1,0:T(8,...) custom-call(s32[16]{0:T(128)S(1)} %broadcast_select_fusion.dst, ...), custom_call_target="tpu_custom_call" | custom-call | flops 12000000000 | bytes 16000000 | tf_op jit(solution)/shard_map/attn_fwd/pallas_call | solution.py:97
  72.9 1.4 copy-done.4
  79.6 34.4 %ffn.1 = (bf16[256,512]{1,0:T(8,128)(2,1)}, bf16[256,512]{1,0:T(8,128)(2,1)}, bf16[256,512]{1,0:T(8,128)(2,1)}, bf16[256,512]{1,0:T(8,128)(2,1)}, f32[1024,512]{...) custom-call(s32[16]{0:T(128)} %copy-done.3, ...), custom_call_target="tpu_custom_call" | custom-call | flops 15000000512 | bytes 20000000 | tf_op jit(solution)/shard_map/ffn/pallas_call | solution.py:252
  114.1 4.9 %collective-permute-done.29 = bf16[2,16,304,128]{3,2,1,0:T(8,128)(2,1)S(1)} collective-permute-done((bf16[2,16,304,128]{3,2,1,0:T(8,128)(2,1)}, bf16[2,16,304,128]{3,2,1,0:T(8,128)(2,1)S(1)}, u32[]{:S(2)}, u32[]{:S(2)}) %collective-permute-start.29) | collective-permute-done | bytes 2490400 | tf_op jit(solution)/shard_map/ppermute | solution.py:397
  119.1 2.3 add_convert_fusion.1
  121.4 1.6 collective-permute-start.30
  123.0 1.6 collective-permute-start.32
  124.6 13.0 %collective-permute-done.30 = bf16[8,304,128]{2,1,0:T(8,128)(2,1)S(1)} collective-permute-done((bf16[8,304,128]{2,1,0:T(8,128)(2,1)S(1)}, bf16[8,304,128]{2,1,0:T(8,128)(2,1)S(1)}, u32[]{:S(2)}, u32[]{:S(2)}) %collective-permute-start.30) | collective-permute-done | bytes 622624 | tf_op jit(solution)/shard_map/ppermute | solution.py:397
  137.8 1.6 collective-permute-start.31
  139.5 1.6 collective-permute-start.33
  141.1 5.3 %collective-permute-done.31 = bf16[4,304,128]{2,1,0:T(8,128)(2,1)S(1)} collective-permute-done((bf16[4,304,128]{2,1,0:T(8,128)(2,1)S(1)}, bf16[4,304,128]{2,1,0:T(8,128)(2,1)S(1)}, u32[]{:S(2)}, u32[]{:S(2)}) %collective-permute-start.31) | collective-permute-done | bytes 311328 | tf_op jit(solution)/shard_map/ppermute | solution.py:397
  146.5 1.4 collective-permute-done.33
  148.1 6.2 %collective-permute-start.34 = (bf16[2,2,304,128]{3,2,0,1:T(8,128)(2,1)S(1)}, bf16[2,2,304,128]{3,2,0,1:T(8,128)(2,1)S(1)}, u32[]{:S(2)}, u32[]{:S(2)}) collective-permute-start(bf16[2,2,304,128]{3,2,0,1:T(8,128)(2,1)S(1)} %bitcast.166), channel_id=1, source_target_pairs={{0,1},{1,0},{2,3},{3,2},{4,5},{5,4},{6,7},{7,6},{8,9},{9,8},{10,11... | collective-permute-start | bytes 933896 | tf_op jit(solution)/shard_map/ppermute | solution.py:400
  154.3 34.6 %attn_bwd.1 = (bf16[256,512]{1,0:T(8,128)(2,1)}, bf16[256,512]{1,0:T(8,128)(2,1)}, bf16[256,512]{1,0:T(8,128)(2,1)}, bf16[256,512]{1,0:T(8,128)(2,1)}, bf16[2,16...) custom-call(s32[16]{0:T(128)} %copy-done.3, s32[3]{0:T(128)} %pad_add_fusion.2.me, f32[16]{0:T(128)} %copy-done.2, ...), custom_call_target="tpu_custom_call" | custom-call | flops 17999998976 | bytes 20000000 | tf_op jit(solution)/shard_map/attn_bwd/pallas_call | solution.py:332
  189.1 1.9 collective-permute-start.35
  191.7 8.1 %collective-permute-done.35 = bf16[2,304,128]{2,1,0:T(8,128)(2,1)S(1)} collective-permute-done((bf16[2,304,128]{2,1,0:T(8,128)(2,1)S(1)}, bf16[2,304,128]{2,1,0:T(8,128)(2,1)S(1)}, u32[]{:S(2)}, u32[]{:S(2)}) %collective-permute-start.35) | collective-permute-done | bytes 155680 | tf_op jit(solution)/shard_map/ppermute | solution.py:400
  200.0 1.6 collective-permute-start.16
  201.6 8.3 %collective-permute-done.36 = bf16[2,304,128]{2,1,0:T(8,128)(2,1)S(1)} collective-permute-done((bf16[2,304,128]{2,1,0:T(8,128)(2,1)S(1)}, bf16[2,304,128]{2,1,0:T(8,128)(2,1)S(1)}, u32[]{:S(2)}, u32[]{:S(2)}) %collective-permute-start.36) | collective-permute-done | bytes 155680 | tf_op jit(solution)/shard_map/ppermute | solution.py:400
  212.2 6.5 %collective-permute-done.37 = bf16[2,2,304,128]{3,2,1,0:T(8,128)(2,1)S(1)} collective-permute-done((bf16[2,2,304,128]{3,2,1,0:T(8,128)(2,1)S(1)}, bf16[2,2,304,128]{3,2,1,0:T(8,128)(2,1)S(1)}, u32[]{:S(2)}, u32[]{:S(2)}) %collective-permute-start.37) | collective-permute-done | bytes 311328 | tf_op jit(solution)/shard_map/ppermute | solution.py:400
  218.8 1.6 collective-permute-start.40
  222.1 5.7 %collective-permute-done.40 = bf16[4,304,128]{2,1,0:T(8,128)(2,1)S(1)} collective-permute-done((bf16[4,304,128]{2,1,0:T(8,128)(2,1)S(1)}, bf16[4,304,128]{2,1,0:T(8,128)(2,1)S(1)}, u32[]{:S(2)}, u32[]{:S(2)}) %collective-permute-start.40) | collective-permute-done | bytes 311328 | tf_op jit(solution)/shard_map/ppermute | solution.py:397
  229.5 1.6 collective-permute-start.39
  231.5 4.3 %collective-permute-done.20 = bf16[2,2,96,128]{3,2,0,1:T(8,128)(2,1)S(1)} collective-permute-done((bf16[2,2,96,128]{3,2,0,1:T(8,128)(2,1)S(1)}, bf16[2,2,96,128]{3,2,0,1:T(8,128)(2,1)S(1)}, u32[]{:S(2)}, u32[]{:S(2)}) %collective-permute-start.20) | collective-permute-done | bytes 98336 | tf_op jit(solution)/shard_map/ppermute | solution.py:400
  235.9 5.8 %collective-permute-done.41 = bf16[8,304,128]{2,1,0:T(8,128)(2,1)S(1)} collective-permute-done((bf16[8,304,128]{2,1,0:T(8,128)(2,1)S(1)}, bf16[8,304,128]{2,1,0:T(8,128)(2,1)S(1)}, u32[]{:S(2)}, u32[]{:S(2)}) %collective-permute-start.41) | collective-permute-done | bytes 622624 | tf_op jit(solution)/shard_map/ppermute | solution.py:397
  242.6 1.7 collective-permute-start.21
  244.4 4.4 %collective-permute-done.21 = bf16[2,96,128]{2,1,0:T(8,128)(2,1)S(1)} collective-permute-done((bf16[2,96,128]{2,1,0:T(8,128)(2,1)S(1)}, bf16[2,96,128]{2,1,0:T(8,128)(2,1)S(1)}, u32[]{:S(2)}, u32[]{:S(2)}) %collective-permute-start.21) | collective-permute-done | bytes 49184 | tf_op jit(solution)/shard_map/ppermute | solution.py:400
  249.5 4.3 %collective-permute-done.22 = bf16[2,96,128]{2,1,0:T(8,128)(2,1)S(1)} collective-permute-done((bf16[2,96,128]{2,1,0:T(8,128)(2,1)S(1)}, bf16[2,96,128]{2,1,0:T(8,128)(2,1)S(1)}, u32[]{:S(2)}, u32[]{:S(2)}) %collective-permute-start.22) | collective-permute-done | bytes 49184 | tf_op jit(solution)/shard_map/ppermute | solution.py:400
  253.9 4.6 %collective-permute-done.23 = bf16[2,2,96,128]{3,2,1,0:T(8,128)(2,1)S(1)} collective-permute-done((bf16[2,2,96,128]{3,2,1,0:T(8,128)(2,1)S(1)}, bf16[2,2,96,128]{3,2,1,0:T(8,128)(2,1)S(1)}, u32[]{:S(2)}, u32[]{:S(2)}) %collective-permute-start.23) | collective-permute-done | bytes 98336 | tf_op jit(solution)/shard_map/ppermute | solution.py:400
  258.6 1.6 collective-permute-start.26
  260.9 2.4 collective-permute-done.26
  264.4 1.5 collective-permute-done.24
  267.3 1.4 collective-permute-start.14
  271.6 1.4 collective-permute-start.10
  273.1 12.9 %collective-permute-done.13 = bf16[256,512]{1,0:T(8,128)(2,1)S(1)} collective-permute-done((bf16[256,512]{1,0:T(8,128)(2,1)}, bf16[256,512]{1,0:T(8,128)(2,1)S(1)}, u32[]{:S(2)}, u32[]{:S(2)}) %collective-permute-start.13) | collective-permute-done | bytes 262176 | tf_op jit(solution)/shard_map/ppermute | solution.py:448
  287.2 13.4 %collective-permute-start.9 = (bf16[256,512]{1,0:T(8,128)(2,1)S(1)}, bf16[256,512]{1,0:T(8,128)(2,1)S(1)}, u32[]{:S(2)}, u32[]{:S(2)}) collective-permute-start(bf16[256,512]{1,0:T(8,128)(2,1)S(1)} %copy-done.18), channel_id=1, source_target_pairs={{0,1},{1,0},{2,3},{3,2},{4,5},{5,4},{6,7},{7,6},{8,9},{9,8},{10,11... | collective-permute-start | bytes 786440 | tf_op jit(solution)/shard_map/ppermute | solution.py:448
  301.6 4.1 %collective-permute-done.10 = bf16[256,512]{1,0:T(8,128)(2,1)S(1)} collective-permute-done((bf16[256,512]{1,0:T(8,128)(2,1)}, bf16[256,512]{1,0:T(8,128)(2,1)S(1)}, u32[]{:S(2)}, u32[]{:S(2)}) %collective-permute-start.10) | collective-permute-done | bytes 262176 | tf_op jit(solution)/shard_map/ppermute | solution.py:448
  305.7 5.4 %collective-permute-done.9 = bf16[256,512]{1,0:T(8,128)(2,1)S(1)} collective-permute-done((bf16[256,512]{1,0:T(8,128)(2,1)S(1)}, bf16[256,512]{1,0:T(8,128)(2,1)S(1)}, u32[]{:S(2)}, u32[]{:S(2)}) %collective-permute-start.9) | collective-permute-done | bytes 262176 | tf_op jit(solution)/shard_map/ppermute | solution.py:448
  312.9 1.3 maximum_convert_fusion
  314.2 11.1 %finish_qkv.1 = (f32[512,512]{1,0:T(8,128)}, f32[512,512]{1,0:T(8,128)}, f32[512,512]{1,0:T(8,128)}) custom-call(s32[2,32]{1,0:T(2,128)S(1)} %iota_xor_fusion.slots, bf16[2,16,96,128]{3,2,1,0:T(8,128)(2,1)S(1)} %pad_maximum_fusion.2.own_a.own_b, bf16[2,16,96,128]{3,2,1,0:T(8,128)(2,1)S(1)} %collective-permute-done.28.other_a.other_b, ...), custom_call_target="tpu_custom_call" | custom-call | tf_op jit(solution)/shard_map/finish_qkv/pallas_call | solution.py:373
  325.3 19.4 %finish_dense.1 = (f32[512,2048]{1,0:T(8,128)}, f32[2048,512]{1,0:T(8,128)}, f32[512,512]{1,0:T(8,128)}, f32[32,16,128]{2,1,0:T(8,128)S(1)}) custom-call(s32[2,32]{1,0:T(2,128)S(1)} %iota_xor_fusion.slots, bf16[2,16,304,128]{3,2,1,0:T(8,128)(2,1)S(1)} %pad_maximum_fusion.own_a.own_b, bf16[2,16,304,128]{3,2,1,0:T(8,128)(2,1)} %collective-permute-done.42.other_a.other_b, ...), custom_call_target="tpu_custom_call" | custom-call | tf_op jit(solution)/shard_map/finish_dense/pallas_call | solution.py:373
  (161 shorter events, 34.5 us)
Async XLA Ops:
  2.8 15.5 %collective-permute-start.2 = (s32[2,128]{1,0:T(2,128)S(1)}, s32[2,128]{1,0:T(2,128)S(1)}, u32[]{:S(2)}, u32[]{:S(2)}) collective-permute-start(s32[2,128]{1,0:T(2,128)S(1)} %get-tuple-element.113), channel_id=1, source_target_pairs={{0,3},{1,2},{2,1},{3,0},{4,7},{5,6},{6,5},{7,4},{8,11},{9,10},{10,... | collective-permute-start | bytes 3080 | tf_op jit(solution)/shard_map/ppermute | solution.py:434
  7.9 10.5 %collective-permute-start.1 = (s32[2,128]{1,0:T(2,128)S(1)}, s32[2,128]{1,0:T(2,128)S(1)}, u32[]{:S(2)}, u32[]{:S(2)}) collective-permute-start(s32[2,128]{1,0:T(2,128)S(1)} %get-tuple-element.114), channel_id=1, source_target_pairs={{0,2},{1,3},{2,0},{3,1},{4,6},{5,7},{6,4},{7,5},{8,10},{9,11},{10,... | collective-permute-start | bytes 3080 | tf_op jit(solution)/shard_map/ppermute | solution.py:434
  7.9 11.1 %collective-permute-start = (s32[2,128]{1,0:T(2,128)S(1)}, s32[2,128]{1,0:T(2,128)S(1)}, u32[]{:S(2)}, u32[]{:S(2)}) collective-permute-start(s32[2,128]{1,0:T(2,128)S(1)} %get-tuple-element.115), channel_id=1, source_target_pairs={{0,1},{1,0},{2,3},{3,2},{4,5},{5,4},{6,7},{7,6},{8,9},{9,8},{10,11... | collective-permute-start | bytes 3080 | tf_op jit(solution)/shard_map/ppermute | solution.py:434
  11.1 67.8 %collective-permute-start.3 = (bf16[256,512]{1,0:T(8,128)(2,1)}, bf16[256,512]{1,0:T(8,128)(2,1)}, u32[]{:S(2)}, u32[]{:S(2)}) collective-permute-start(bf16[256,512]{1,0:T(8,128)(2,1)} %get-tuple-element.96), channel_id=1, source_target_pairs={{0,1},{1,0},{2,3},{3,2},{4,5},{5,4},{6,7},{7,6},{8,9},{9,8},{10,11... | collective-permute-start | bytes 786440 | tf_op jit(solution)/shard_map/ppermute | solution.py:434
  12.5 66.4 %collective-permute-start.4 = (bf16[256,512]{1,0:T(8,128)(2,1)}, bf16[256,512]{1,0:T(8,128)(2,1)}, u32[]{:S(2)}, u32[]{:S(2)}) collective-permute-start(bf16[256,512]{1,0:T(8,128)(2,1)} %get-tuple-element.97), channel_id=1, source_target_pairs={{0,2},{1,3},{2,0},{3,1},{4,6},{5,7},{6,4},{7,5},{8,10},{9,11},{10,... | collective-permute-start | bytes 786440 | tf_op jit(solution)/shard_map/ppermute | solution.py:434
  16.8 33.4 %copy-start = (bf16[512,1536]{1,0:T(8,128)(2,1)}, bf16[512,1536]{1,0:T(8,128)(2,1)S(1)}, u32[]{:S(2)}) copy-start(bf16[512,1536]{1,0:T(8,128)(2,1)S(1)} %constant_dynamic-update-slice_fusion.w) | copy-start | bytes 4718596
  17.6 32.6 %copy-start.2 = (f32[16]{0:T(128)}, f32[16]{0:T(128)S(1)}, u32[]{:S(2)}) copy-start(f32[16]{0:T(128)S(1)} %select_n.224.bias) | copy-start | bytes 196
  18.3 16.8 %collective-permute-start.6 = (bf16[256,512]{1,0:T(8,128)(2,1)}, bf16[256,512]{1,0:T(8,128)(2,1)}, u32[]{:S(2)}, u32[]{:S(2)}) collective-permute-start(bf16[256,512]{1,0:T(8,128)(2,1)} %get-tuple-element.92), channel_id=1, source_target_pairs={{0,1},{1,0},{2,3},{3,2},{4,5},{5,4},{6,7},{7,6},{8,9},{9,8},{10,11... | collective-permute-start | bytes 786440 | tf_op jit(solution)/shard_map/ppermute | solution.py:434
  18.4 31.8 %collective-permute-start.7 = (bf16[256,512]{1,0:T(8,128)(2,1)}, bf16[256,512]{1,0:T(8,128)(2,1)}, u32[]{:S(2)}, u32[]{:S(2)}) collective-permute-start(bf16[256,512]{1,0:T(8,128)(2,1)} %get-tuple-element.93), channel_id=1, source_target_pairs={{0,2},{1,3},{2,0},{3,1},{4,6},{5,7},{6,4},{7,5},{8,10},{9,11},{10,... | collective-permute-start | bytes 786440 | tf_op jit(solution)/shard_map/ppermute | solution.py:434
  19.0 31.2 %collective-permute-start.8 = (bf16[256,512]{1,0:T(8,128)(2,1)}, bf16[256,512]{1,0:T(8,128)(2,1)}, u32[]{:S(2)}, u32[]{:S(2)}) collective-permute-start(bf16[256,512]{1,0:T(8,128)(2,1)} %get-tuple-element.90), channel_id=1, source_target_pairs={{0,3},{1,2},{2,1},{3,0},{4,7},{5,6},{6,5},{7,4},{8,11},{9,10},{10,... | collective-permute-start | bytes 786440 | tf_op jit(solution)/shard_map/ppermute | solution.py:434
  23.0 49.9 %copy-start.3 = (s32[16]{0:T(128)}, s32[16]{0:T(128)S(1)}, u32[]{:S(2)}) copy-start(s32[16]{0:T(128)S(1)} %broadcast_select_fusion.dst) | copy-start | bytes 196
  23.5 49.5 %copy-start.1 = (f32[4,256,256]{2,1,0:T(8,128)}, f32[4,256,256]{2,1,0:T(8,128)S(1)}, u32[]{:S(2)}) copy-start(f32[4,256,256]{2,1,0:T(8,128)S(1)} %compare_select_fusion.mask) | copy-start | bytes 3145732
  35.1 43.8 %collective-permute-start.5 = (bf16[256,512]{1,0:T(8,128)(2,1)}, bf16[256,512]{1,0:T(8,128)(2,1)S(1)}, u32[]{:S(2)}, u32[]{:S(2)}) collective-permute-start(bf16[256,512]{1,0:T(8,128)(2,1)} %get-tuple-element.94), channel_id=1, source_target_pairs={{0,3},{1,2},{2,1},{3,0},{4,7},{5,6},{6,5},{7,4},{8,11},{9,10},{10,... | collective-permute-start | bytes 786440 | tf_op jit(solution)/shard_map/ppermute | solution.py:434
  114.1 5.0 %collective-permute-start.29 = (bf16[2,16,304,128]{3,2,1,0:T(8,128)(2,1)}, bf16[2,16,304,128]{3,2,1,0:T(8,128)(2,1)S(1)}, u32[]{:S(2)}, u32[]{:S(2)}) collective-permute-start(bf16[2,16,304,128]{3,2,1,0:T(8,128)(2,1)} %get-tuple-element.73), channel_id=1, source_target_pairs={{0,4},{4,0},{8,12},{12,8},{16,20},{20,16},{24,28},{28,24},{1,5},{5... | collective-permute-start | bytes 7471112 | tf_op jit(solution)/shard_map/ppermute | solution.py:397
  121.4 16.1 %collective-permute-start.30 = (bf16[8,304,128]{2,1,0:T(8,128)(2,1)S(1)}, bf16[8,304,128]{2,1,0:T(8,128)(2,1)S(1)}, u32[]{:S(2)}, u32[]{:S(2)}) collective-permute-start(bf16[8,304,128]{2,1,0:T(8,128)(2,1)S(1)} %slice_bitcast_fusion.2), channel_id=1, source_target_pairs={{0,8},{4,12},{8,0},{12,4},{16,24},{20,28},{24,16},{28,20},{1,9},{5... | collective-permute-start | bytes 1867784 | tf_op jit(solution)/shard_map/ppermute | solution.py:397
  123.0 16.3 %collective-permute-start.32 = (bf16[8,304,128]{2,1,0:T(8,128)(2,1)S(1)}, bf16[8,304,128]{2,1,0:T(8,128)(2,1)S(1)}, u32[]{:S(2)}, u32[]{:S(2)}) collective-permute-start(bf16[8,304,128]{2,1,0:T(8,128)(2,1)S(1)} %slice_bitcast_fusion), channel_id=1, source_target_pairs={{0,16},{4,20},{8,24},{12,28},{16,0},{20,4},{24,8},{28,12},{1,17},{... | collective-permute-start | bytes 1867784 | tf_op jit(solution)/shard_map/ppermute | solution.py:397
  137.8 8.6 %collective-permute-start.31 = (bf16[4,304,128]{2,1,0:T(8,128)(2,1)S(1)}, bf16[4,304,128]{2,1,0:T(8,128)(2,1)S(1)}, u32[]{:S(2)}, u32[]{:S(2)}) collective-permute-start(bf16[4,304,128]{2,1,0:T(8,128)(2,1)S(1)} %slice.222), channel_id=1, source_target_pairs={{0,16},{4,20},{8,24},{12,28},{16,0},{20,4},{24,8},{28,12},{1,17},{... | collective-permute-start | bytes 933896 | tf_op jit(solution)/shard_map/ppermute | solution.py:397
  139.5 8.4 %collective-permute-start.33 = (bf16[4,304,128]{2,1,0:T(8,128)(2,1)S(1)}, bf16[4,304,128]{2,1,0:T(8,128)(2,1)S(1)}, u32[]{:S(2)}, u32[]{:S(2)}) collective-permute-start(bf16[4,304,128]{2,1,0:T(8,128)(2,1)S(1)} %slice.227), channel_id=1, source_target_pairs={{0,8},{4,12},{8,0},{12,4},{16,24},{20,28},{24,16},{28,20},{1,9},{5... | collective-permute-start | bytes 933896 | tf_op jit(solution)/shard_map/ppermute | solution.py:397
  148.1 41.0 %collective-permute-start.34 = (bf16[2,2,304,128]{3,2,0,1:T(8,128)(2,1)S(1)}, bf16[2,2,304,128]{3,2,0,1:T(8,128)(2,1)S(1)}, u32[]{:S(2)}, u32[]{:S(2)}) collective-permute-start(bf16[2,2,304,128]{3,2,0,1:T(8,128)(2,1)S(1)} %bitcast.166), channel_id=1, source_target_pairs={{0,1},{1,0},{2,3},{3,2},{4,5},{5,4},{6,7},{7,6},{8,9},{9,8},{10,11... | collective-permute-start | bytes 933896 | tf_op jit(solution)/shard_map/ppermute | solution.py:400
  188.9 2.6 collective-permute-start.15
  189.1 10.7 %collective-permute-start.35 = (bf16[2,304,128]{2,1,0:T(8,128)(2,1)S(1)}, bf16[2,304,128]{2,1,0:T(8,128)(2,1)S(1)}, u32[]{:S(2)}, u32[]{:S(2)}) collective-permute-start(bf16[2,304,128]{2,1,0:T(8,128)(2,1)S(1)} %slice_bitcast_fusion.8), channel_id=1, source_target_pairs={{0,2},{1,3},{2,0},{3,1},{4,6},{5,7},{6,4},{7,5},{8,10},{9,11},{10,... | collective-permute-start | bytes 466952 | tf_op jit(solution)/shard_map/ppermute | solution.py:400
  199.9 9.9 %collective-permute-start.36 = (bf16[2,304,128]{2,1,0:T(8,128)(2,1)S(1)}, bf16[2,304,128]{2,1,0:T(8,128)(2,1)S(1)}, u32[]{:S(2)}, u32[]{:S(2)}) collective-permute-start(bf16[2,304,128]{2,1,0:T(8,128)(2,1)S(1)} %fusion.7), channel_id=1, source_target_pairs={{0,2},{1,3},{2,0},{3,1},{4,6},{5,7},{6,4},{7,5},{8,10},{9,11},{10,... | collective-permute-start | bytes 466952 | tf_op jit(solution)/shard_map/ppermute | solution.py:400
  200.0 11.1 %collective-permute-start.16 = (bf16[8,96,128]{2,1,0:T(8,128)(2,1)S(1)}, bf16[8,96,128]{2,1,0:T(8,128)(2,1)S(1)}, u32[]{:S(2)}, u32[]{:S(2)}) collective-permute-start(bf16[8,96,128]{2,1,0:T(8,128)(2,1)S(1)} %slice_bitcast_fusion.6), channel_id=1, source_target_pairs={{0,8},{4,12},{8,0},{12,4},{16,24},{20,28},{24,16},{28,20},{1,9},{5... | collective-permute-start | bytes 589832 | tf_op jit(solution)/shard_map/ppermute | solution.py:397
  209.9 8.8 %collective-permute-start.37 = (bf16[2,2,304,128]{3,2,1,0:T(8,128)(2,1)S(1)}, bf16[2,2,304,128]{3,2,1,0:T(8,128)(2,1)S(1)}, u32[]{:S(2)}, u32[]{:S(2)}) collective-permute-start(bf16[2,2,304,128]{3,2,1,0:T(8,128)(2,1)S(1)} %get-tuple-element.103), channel_id=1, source_target_pairs={{0,1},{1,0},{2,3},{3,2},{4,5},{5,4},{6,7},{7,6},{8,9},{9,8},{10,11... | collective-permute-start | bytes 933896 | tf_op jit(solution)/shard_map/ppermute | solution.py:400
  210.0 10.4 %collective-permute-start.18 = (bf16[8,96,128]{2,1,0:T(8,128)(2,1)S(1)}, bf16[8,96,128]{2,1,0:T(8,128)(2,1)S(1)}, u32[]{:S(2)}, u32[]{:S(2)}) collective-permute-start(bf16[8,96,128]{2,1,0:T(8,128)(2,1)S(1)} %slice_bitcast_fusion.4), channel_id=1, source_target_pairs={{0,16},{4,20},{8,24},{12,28},{16,0},{20,4},{24,8},{28,12},{1,17},{... | collective-permute-start | bytes 589832 | tf_op jit(solution)/shard_map/ppermute | solution.py:397
  211.2 10.9 %collective-permute-start.17 = (bf16[4,96,128]{2,1,0:T(8,128)(2,1)S(1)}, bf16[4,96,128]{2,1,0:T(8,128)(2,1)S(1)}, u32[]{:S(2)}, u32[]{:S(2)}) collective-permute-start(bf16[4,96,128]{2,1,0:T(8,128)(2,1)S(1)} %slice.206), channel_id=1, source_target_pairs={{0,16},{4,20},{8,24},{12,28},{16,0},{20,4},{24,8},{28,12},{1,17},{... | collective-permute-start | bytes 294920 | tf_op jit(solution)/shard_map/ppermute | solution.py:397
  218.8 9.0 %collective-permute-start.40 = (bf16[4,304,128]{2,1,0:T(8,128)(2,1)S(1)}, bf16[4,304,128]{2,1,0:T(8,128)(2,1)S(1)}, u32[]{:S(2)}, u32[]{:S(2)}) collective-permute-start(bf16[4,304,128]{2,1,0:T(8,128)(2,1)S(1)} %bitcast.151), channel_id=1, source_target_pairs={{0,8},{4,12},{8,0},{12,4},{16,24},{20,28},{24,16},{28,20},{1,9},{5... | collective-permute-start | bytes 933896 | tf_op jit(solution)/shard_map/ppermute | solution.py:397
  220.4 10.7 %collective-permute-start.19 = (bf16[4,96,128]{2,1,0:T(8,128)(2,1)S(1)}, bf16[4,96,128]{2,1,0:T(8,128)(2,1)S(1)}, u32[]{:S(2)}, u32[]{:S(2)}) collective-permute-start(bf16[4,96,128]{2,1,0:T(8,128)(2,1)S(1)} %slice.211), channel_id=1, source_target_pairs={{0,8},{4,12},{8,0},{12,4},{16,24},{20,28},{24,16},{28,20},{1,9},{5... | collective-permute-start | bytes 294920 | tf_op jit(solution)/shard_map/ppermute | solution.py:397
  221.0 8.4 %collective-permute-start.38 = (bf16[4,304,128]{2,1,0:T(8,128)(2,1)S(1)}, bf16[4,304,128]{2,1,0:T(8,128)(2,1)S(1)}, u32[]{:S(2)}, u32[]{:S(2)}) collective-permute-start(bf16[4,304,128]{2,1,0:T(8,128)(2,1)S(1)} %bitcast.148), channel_id=1, source_target_pairs={{0,16},{4,20},{8,24},{12,28},{16,0},{20,4},{24,8},{28,12},{1,17},{... | collective-permute-start | bytes 933896 | tf_op jit(solution)/shard_map/ppermute | solution.py:397
  227.8 13.8 %collective-permute-start.41 = (bf16[8,304,128]{2,1,0:T(8,128)(2,1)S(1)}, bf16[8,304,128]{2,1,0:T(8,128)(2,1)S(1)}, u32[]{:S(2)}, u32[]{:S(2)}) collective-permute-start(bf16[8,304,128]{2,1,0:T(8,128)(2,1)S(1)} %pad_maximum_fusion.4), channel_id=1, source_target_pairs={{0,16},{4,20},{8,24},{12,28},{16,0},{20,4},{24,8},{28,12},{1,17},{... | collective-permute-start | bytes 1867784 | tf_op jit(solution)/shard_map/ppermute | solution.py:397
  229.5 12.6 %collective-permute-start.39 = (bf16[8,304,128]{2,1,0:T(8,128)(2,1)S(1)}, bf16[8,304,128]{2,1,0:T(8,128)(2,1)S(1)}, u32[]{:S(2)}, u32[]{:S(2)}) collective-permute-start(bf16[8,304,128]{2,1,0:T(8,128)(2,1)S(1)} %pad_maximum_fusion.3), channel_id=1, source_target_pairs={{0,8},{4,12},{8,0},{12,4},{16,24},{20,28},{24,16},{28,20},{1,9},{5... | collective-permute-start | bytes 1867784 | tf_op jit(solution)/shard_map/ppermute | solution.py:397
  231.2 4.7 %collective-permute-start.20 = (bf16[2,2,96,128]{3,2,0,1:T(8,128)(2,1)S(1)}, bf16[2,2,96,128]{3,2,0,1:T(8,128)(2,1)S(1)}, u32[]{:S(2)}, u32[]{:S(2)}) collective-permute-start(bf16[2,2,96,128]{3,2,0,1:T(8,128)(2,1)S(1)} %bitcast.173), channel_id=1, source_target_pairs={{0,1},{1,0},{2,3},{3,2},{4,5},{5,4},{6,7},{7,6},{8,9},{9,8},{10,11... | collective-permute-start | bytes 294920 | tf_op jit(solution)/shard_map/ppermute | solution.py:400
  242.5 82.7 %collective-permute-start.42 = (bf16[2,16,304,128]{3,2,1,0:T(8,128)(2,1)S(1)}, bf16[2,16,304,128]{3,2,1,0:T(8,128)(2,1)}, u32[]{:S(2)}, u32[]{:S(2)}) collective-permute-start(bf16[2,16,304,128]{3,2,1,0:T(8,128)(2,1)S(1)} %pad_maximum_fusion.own_a.own_b), channel_id=1, source_target_pairs={{0,4},{4,0},{8,12},{12,8},{16,20},{20,16},{24,28},{28,24},{1,5},{5... | collective-permute-start | bytes 7471112 | tf_op jit(solution)/shard_map/ppermute | solution.py:397
  242.6 6.1 %collective-permute-start.21 = (bf16[2,96,128]{2,1,0:T(8,128)(2,1)S(1)}, bf16[2,96,128]{2,1,0:T(8,128)(2,1)S(1)}, u32[]{:S(2)}, u32[]{:S(2)}) collective-permute-start(bf16[2,96,128]{2,1,0:T(8,128)(2,1)S(1)} %slice_bitcast_fusion.10), channel_id=1, source_target_pairs={{0,2},{1,3},{2,0},{3,1},{4,6},{5,7},{6,4},{7,5},{8,10},{9,11},{10,... | collective-permute-start | bytes 147464 | tf_op jit(solution)/shard_map/ppermute | solution.py:400
  248.7 5.1 %collective-permute-start.22 = (bf16[2,96,128]{2,1,0:T(8,128)(2,1)S(1)}, bf16[2,96,128]{2,1,0:T(8,128)(2,1)S(1)}, u32[]{:S(2)}, u32[]{:S(2)}) collective-permute-start(bf16[2,96,128]{2,1,0:T(8,128)(2,1)S(1)} %fusion.27), channel_id=1, source_target_pairs={{0,2},{1,3},{2,0},{3,1},{4,6},{5,7},{6,4},{7,5},{8,10},{9,11},{10,... | collective-permute-start | bytes 147464 | tf_op jit(solution)/shard_map/ppermute | solution.py:400
  253.9 4.7 %collective-permute-start.23 = (bf16[2,2,96,128]{3,2,1,0:T(8,128)(2,1)S(1)}, bf16[2,2,96,128]{3,2,1,0:T(8,128)(2,1)S(1)}, u32[]{:S(2)}, u32[]{:S(2)}) collective-permute-start(bf16[2,2,96,128]{3,2,1,0:T(8,128)(2,1)S(1)} %get-tuple-element.111), channel_id=1, source_target_pairs={{0,1},{1,0},{2,3},{3,2},{4,5},{5,4},{6,7},{7,6},{8,9},{9,8},{10,11... | collective-permute-start | bytes 294920 | tf_op jit(solution)/shard_map/ppermute | solution.py:400
  258.6 4.7 %collective-permute-start.26 = (bf16[4,96,128]{2,1,0:T(8,128)(2,1)S(1)}, bf16[4,96,128]{2,1,0:T(8,128)(2,1)S(1)}, u32[]{:S(2)}, u32[]{:S(2)}) collective-permute-start(bf16[4,96,128]{2,1,0:T(8,128)(2,1)S(1)} %bitcast.160), channel_id=1, source_target_pairs={{0,8},{4,12},{8,0},{12,4},{16,24},{20,28},{24,16},{28,20},{1,9},{5... | collective-permute-start | bytes 294920 | tf_op jit(solution)/shard_map/ppermute | solution.py:397
  260.2 5.6 %collective-permute-start.24 = (bf16[4,96,128]{2,1,0:T(8,128)(2,1)S(1)}, bf16[4,96,128]{2,1,0:T(8,128)(2,1)S(1)}, u32[]{:S(2)}, u32[]{:S(2)}) collective-permute-start(bf16[4,96,128]{2,1,0:T(8,128)(2,1)S(1)} %bitcast.157), channel_id=1, source_target_pairs={{0,16},{4,20},{8,24},{12,28},{16,0},{20,4},{24,8},{28,12},{1,17},{... | collective-permute-start | bytes 294920 | tf_op jit(solution)/shard_map/ppermute | solution.py:397
  263.3 5.8 %collective-permute-start.27 = (bf16[8,96,128]{2,1,0:T(8,128)(2,1)S(1)}, bf16[8,96,128]{2,1,0:T(8,128)(2,1)}, u32[]{:S(2)}, u32[]{:S(2)}) collective-permute-start(bf16[8,96,128]{2,1,0:T(8,128)(2,1)S(1)} %pad_maximum_fusion.9), channel_id=1, source_target_pairs={{0,16},{4,20},{8,24},{12,28},{16,0},{20,4},{24,8},{28,12},{1,17},{... | collective-permute-start | bytes 589832 | tf_op jit(solution)/shard_map/ppermute | solution.py:397
  265.8 5.7 %collective-permute-start.25 = (bf16[8,96,128]{2,1,0:T(8,128)(2,1)S(1)}, bf16[8,96,128]{2,1,0:T(8,128)(2,1)S(1)}, u32[]{:S(2)}, u32[]{:S(2)}) collective-permute-start(bf16[8,96,128]{2,1,0:T(8,128)(2,1)S(1)} %pad_maximum_fusion.8), channel_id=1, source_target_pairs={{0,8},{4,12},{8,0},{12,4},{16,24},{20,28},{24,16},{28,20},{1,9},{5... | collective-permute-start | bytes 589832 | tf_op jit(solution)/shard_map/ppermute | solution.py:397
  266.2 19.9 %collective-permute-start.13 = (bf16[256,512]{1,0:T(8,128)(2,1)}, bf16[256,512]{1,0:T(8,128)(2,1)S(1)}, u32[]{:S(2)}, u32[]{:S(2)}) collective-permute-start(bf16[256,512]{1,0:T(8,128)(2,1)} %get-tuple-element.65), channel_id=1, source_target_pairs={{0,2},{1,3},{2,0},{3,1},{4,6},{5,7},{6,4},{7,5},{8,10},{9,11},{10,... | collective-permute-start | bytes 786440 | tf_op jit(solution)/shard_map/ppermute | solution.py:448
  267.3 19.9 %collective-permute-start.14 = (bf16[256,512]{1,0:T(8,128)(2,1)}, bf16[256,512]{1,0:T(8,128)(2,1)S(1)}, u32[]{:S(2)}, u32[]{:S(2)}) collective-permute-start(bf16[256,512]{1,0:T(8,128)(2,1)} %get-tuple-element.66), channel_id=1, source_target_pairs={{0,3},{1,2},{2,1},{3,0},{4,7},{5,6},{6,5},{7,4},{8,11},{9,10},{10,... | collective-permute-start | bytes 786440 | tf_op jit(solution)/shard_map/ppermute | solution.py:448
  269.1 31.5 %collective-permute-start.12 = (bf16[256,512]{1,0:T(8,128)(2,1)}, bf16[256,512]{1,0:T(8,128)(2,1)S(1)}, u32[]{:S(2)}, u32[]{:S(2)}) collective-permute-start(bf16[256,512]{1,0:T(8,128)(2,1)} %get-tuple-element.64), channel_id=1, source_target_pairs={{0,1},{1,0},{2,3},{3,2},{4,5},{5,4},{6,7},{7,6},{8,9},{9,8},{10,11... | collective-permute-start | bytes 786440 | tf_op jit(solution)/shard_map/ppermute | solution.py:448
  271.6 34.1 %collective-permute-start.10 = (bf16[256,512]{1,0:T(8,128)(2,1)}, bf16[256,512]{1,0:T(8,128)(2,1)S(1)}, u32[]{:S(2)}, u32[]{:S(2)}) collective-permute-start(bf16[256,512]{1,0:T(8,128)(2,1)} %get-tuple-element.51), channel_id=1, source_target_pairs={{0,2},{1,3},{2,0},{3,1},{4,6},{5,7},{6,4},{7,5},{8,10},{9,11},{10,... | collective-permute-start | bytes 786440 | tf_op jit(solution)/shard_map/ppermute | solution.py:448
  273.1 38.0 %copy-start.16 = (bf16[256,512]{1,0:T(8,128)(2,1)S(1)}, bf16[256,512]{1,0:T(8,128)(2,1)}, u32[]{:S(2)}) copy-start(bf16[256,512]{1,0:T(8,128)(2,1)} %get-tuple-element.49) | copy-start | bytes 786436
  286.0 19.7 %collective-permute-start.11 = (bf16[256,512]{1,0:T(8,128)(2,1)S(1)}, bf16[256,512]{1,0:T(8,128)(2,1)S(1)}, u32[]{:S(2)}, u32[]{:S(2)}) collective-permute-start(bf16[256,512]{1,0:T(8,128)(2,1)S(1)} %copy-done.19), channel_id=1, source_target_pairs={{0,3},{1,2},{2,1},{3,0},{4,7},{5,6},{6,5},{7,4},{8,11},{9,10},{10,... | collective-permute-start | bytes 786440 | tf_op jit(solution)/shard_map/ppermute | solution.py:448
  287.2 23.9 %collective-permute-start.9 = (bf16[256,512]{1,0:T(8,128)(2,1)S(1)}, bf16[256,512]{1,0:T(8,128)(2,1)S(1)}, u32[]{:S(2)}, u32[]{:S(2)}) collective-permute-start(bf16[256,512]{1,0:T(8,128)(2,1)S(1)} %copy-done.18), channel_id=1, source_target_pairs={{0,1},{1,0},{2,3},{3,2},{4,5},{5,4},{6,7},{7,6},{8,9},{9,8},{10,11... | collective-permute-start | bytes 786440 | tf_op jit(solution)/shard_map/ppermute | solution.py:448
  300.6 13.6 %collective-permute-start.28 = (bf16[2,16,96,128]{3,2,1,0:T(8,128)(2,1)S(1)}, bf16[2,16,96,128]{3,2,1,0:T(8,128)(2,1)S(1)}, u32[]{:S(2)}, u32[]{:S(2)}) collective-permute-start(bf16[2,16,96,128]{3,2,1,0:T(8,128)(2,1)S(1)} %pad_maximum_fusion.2.own_a.own_b), channel_id=1, source_target_pairs={{0,4},{4,0},{8,12},{12,8},{16,20},{20,16},{24,28},{28,24},{1,5},{5... | collective-permute-start | bytes 2359304 | tf_op jit(solution)/shard_map/ppermute | solution.py:397
  (16 other events, 107.1 us)
